TPU v7x, 128 devices: a whole 4x4x4 slice. The times are simulated.
128 devices in a mesh: dp: 32 (over x, z, core), rows: 4 (over y).
Axes of the slice: x: 4, y: 4, z: 4, core: 2. Of those that a mesh axis runs over, the one named last changes fastest.
Arguments:
- images: bfloat16 [192, 32, 128, 256], P('dp', 'rows'), may hold values from -120 to 120
- kernel: bfloat16 [3, 3, 256, 128], replicated, may hold values from -0.25 to 0.25
- colors: float32 [2, 64, 64], replicated, may hold values from -0.75 to 0.75
- offset: float32 [128], replicated, may hold values from -4 to 4
- upstream: bfloat16 [192, 32, 128, 128], P('dp', 'rows'), may hold values from -8 to 8
Outputs:
- colored: bfloat16 [192, 32, 128, 128], P('dp', 'rows')
- grad_images: bfloat16 [192, 32, 128, 256], P('dp', 'rows')
- grad_kernel: float32 [3, 3, 256, 128], replicated
- grad_colors: float32 [2, 64, 64], replicated
All inputs are finite; a program needn't handle non-finite values.
Results may differ from a plain program's by a relative error of at most 0.0044.
The roundings to bfloat16 on the way count: a program that leaves them out, or rounds other values in their place, can miss the bound.
Values may be sent and summed in bfloat16 or wider, within the bound.
A program may use at most 128 MiB of HBM per device.

v0:
```python
import math

import jax
import jax.numpy as jnp
from jax import lax
from jax.sharding import PartitionSpec as P

NS_ITERS = 5


EPSILON = 1e-05
PRECISE = lax.Precision.HIGHEST


def with_halo(block, sides, width):
    for axis, dim in sides:
        count = lax.axis_size(axis)
        forward = [(i, i + 1) for i in range(count - 1)]
        backward = [(target, source) for source, target in forward]
        low = lax.ppermute(
            lax.slice_in_dim(block, block.shape[dim] - width, None, axis=dim), axis, forward
        )
        high = lax.ppermute(lax.slice_in_dim(block, 0, width, axis=dim), axis, backward)
        block = jnp.concatenate([low, block, high], axis=dim)
    return block


def batched(left, right):
    return jnp.einsum("gij,gjk->gik", left, right, precision=PRECISE)


def inv_root(sigma_mat):
    traces = jnp.trace(sigma_mat, axis1=1, axis2=2)
    normed = sigma_mat / traces[:, None, None]
    estimate = jnp.broadcast_to(
        jnp.eye(sigma_mat.shape[-1], dtype=sigma_mat.dtype), sigma_mat.shape
    )
    for repeat in range(NS_ITERS):
        cubed = batched(batched(estimate, estimate), estimate)
        estimate = 1.5 * estimate - 0.5 * batched(cubed, normed)
    return estimate / jnp.sqrt(traces)[:, None, None]


def filter_valid(source, weights):
    return lax.conv_general_dilated(
        source,
        weights,
        (1, 1),
        "VALID",
        dimension_numbers=("NHWC", "HWIO", "NHWC"),
        preferred_element_type=jnp.float32,
    )


def body(images, kernel, colors, offset, upstream):
    img_count, band_rows, width_n, in_chan = images.shape
    out_chan = kernel.shape[3]
    groups = colors.shape[0]
    group_size = colors.shape[1]
    total_pix = img_count * band_rows * width_n * lax.axis_size("dp") * lax.axis_size("rows")
    rimmed = with_halo(images, (("rows", 1),), 1)
    padded = jnp.pad(rimmed, ((0, 0), (0, 0), (1, 1), (0, 0)))
    pre = filter_valid(padded, kernel)
    raw_cols = pre.reshape(-1, groups, group_size)
    identity = jnp.eye(group_size, dtype=jnp.float32)
    average = lax.psum(jnp.sum(raw_cols, axis=0), ("dp", "rows")) / total_pix
    centred = raw_cols - average
    local_cov = jnp.einsum("pgi,pgj->gij", centred, centred, precision=PRECISE)
    covariance = lax.psum(local_cov, ("dp", "rows")) / total_pix
    sigma_mat = covariance + EPSILON * identity
    whitener, pullback = jax.vjp(inv_root, sigma_mat)
    whitened = jnp.einsum("gij,pgj->pgi", whitener, centred, precision=PRECISE)
    colored = jnp.einsum("gij,pgj->pgi", colors, whitened, precision=PRECISE) + offset.reshape(
        groups, group_size
    )
    colored = colored.astype(jnp.bfloat16).reshape(pre.shape)
    upward = upstream.reshape(-1, groups, group_size).astype(jnp.float32)
    white_grad = jnp.einsum("gji,pgj->pgi", colors, upward, precision=PRECISE)
    local_up = jnp.sum(upward, axis=0)
    local_color = jnp.einsum("pgi,pgj->gij", upward, whitened, precision=PRECISE)
    local_whiten = jnp.einsum("pgi,pgj->gij", white_grad, centred, precision=PRECISE)
    up_total, color_sum, whiten_grad = lax.psum(
        (local_up, local_color, local_whiten), ("dp", "rows")
    )
    (sigma_grad,) = pullback(whiten_grad)
    symmetric = sigma_grad + jnp.transpose(sigma_grad, (0, 2, 1))
    mean_grad = jnp.einsum("gji,gj->gi", colors, up_total, precision=PRECISE) / total_pix
    centred_grad = jnp.einsum("gji,pgj->pgi", whitener, white_grad, precision=PRECISE)
    centred_grad = (
        centred_grad + jnp.einsum("gij,pgj->pgi", symmetric, centred, precision=PRECISE) / total_pix
    )
    pre_grad = centred_grad - jnp.einsum("gji,gj->gi", whitener, mean_grad, precision=PRECISE)
    pre_grad = pre_grad.astype(jnp.bfloat16).reshape(pre.shape)
    grad_rimmed = with_halo(pre_grad, (("rows", 1),), 1)
    grad_padded = jnp.pad(grad_rimmed, ((0, 0), (0, 0), (1, 1), (0, 0)))
    flipped = jnp.transpose(kernel[::-1, ::-1], (0, 1, 3, 2))
    grad_images = filter_valid(grad_padded, flipped).astype(jnp.bfloat16)
    grad_flat = pre_grad.reshape(-1, out_chan)
    outer = []
    for row_off in range(3):
        inner = []
        for col_off in range(3):
            window = padded[
                :, row_off : row_off + band_rows, col_off : col_off + width_n, :
            ].reshape(-1, in_chan)
            inner.append(
                lax.dot_general(
                    window, grad_flat, (((0,), (0,)), ((), ())), preferred_element_type=jnp.float32
                )
            )
        outer.append(jnp.stack(inner))
    kernel_term = jnp.stack(outer)
    summed = lax.psum(kernel_term, ("dp", "rows"))
    scaling = 1.0 / math.sqrt(total_pix)
    return (colored, grad_images, summed * scaling, color_sum * scaling)


def solution(mesh):
    placed = (P("dp", "rows", None, None), P(), P(), P(), P("dp", "rows", None, None))
    return jax.shard_map(
        body,
        mesh=mesh,
        in_specs=placed,
        out_specs=(P("dp", "rows", None, None), P("dp", "rows", None, None), P(), P()),
        check_vma=False,
    )
```

profile of v0, /device:TPU:1, one launch (start us, length us, event | category | flops | bytes accessed | tf_op | source)
XLA Modules:
  0.0 588.7 jit_solution(5691522462129279243)
XLA Ops:
  10.6 4.7 collective-permute-start
  22.7 3.1 convolution_bitcast_fusion
  29.1 6.3 %pad_maximum_fusion.1 = (bf16[6,8,128,256]{3,2,1,0:T(8,128)(2,1)}, bf16[6,8,128,256]{3,2,1,0:T(8,128)(2,1)}, bf16[6,10,128,256]{3,2,1,0:T(8,128)(2,1)S(1)}) fusion(bf16[6,8,128,256]{3,2,1,0:T(8,128)(2,1)} %param.5, bf16[6,1,128,256]{3,2,1,0:T(8,128)(2,1)S(1)} %collective-permute-done, bf16[6,1,128,256]{3,2,1,0:T(8,128)(2,1)S(1)} %collective-permute-done.1, ...), kind=kLoop, calls=%fused_computation.19 | loop fusion | flops 12582912 | bytes 13369344 | tf_op jit(solution)/shard_map/concatenate | solution.py:24
  35.4 13.9 %pad_slice_fusion.5 = (bf16[6,8,128,256]{3,2,1,0:T(8,128)(2,1)}, bf16[6,8,128,256]{3,2,1,0:T(8,128)(2,1)}, bf16[6,8,128,256]{3,2,1,0:T(8,128)(2,1)}, bf16[6,8,12...) fusion(bf16[6,10,128,256]{3,2,1,0:T(8,128)(2,1)S(1)} %constant_dynamic-update-slice_fusion), kind=kLoop, calls=%fused_computation.37 | loop fusion | bytes 22806528 | tf_op jit(solution)/shard_map/slice | solution.py:103
  49.7 4.7 pad.7.clone
  54.4 7.9 %reshape.99 = bf16[10,6,8,17,256]{4,3,2,1,0:T(8,128)(2,1)} reshape(bf16[10,6,136,256]{3,2,1,0:T(8,128)(2,1)} %pad.7.clone) | data formatting | bytes 8355840 | tf_op jit(solution)/shard_map/conv_general_dilated | solution.py:45
  64.0 4.4 fusion.4
  68.4 10.0 %select_reduce_fusion = (f32[128]{0:T(128)S(1)}, f32[8,48,17,128]{3,1,2,0:T(8,128)}) fusion(pred[48,17]{0,1:T(8,128)(4,1)S(1)} %copy-done.21, bf16[3,3,256,128]{3,2,1,0:T(8,128)(2,1)S(1)} %copy-done, bf16[10,6,8,19,256]{4,3,2,1,0:T(8,128)(2,1)S(1)} %fusion.4), kind=kOutput, calls=%fused_computation.17 | convolution fusion | flops 3852877824 | bytes 8602928 | tf_op jit(solution)/shard_map/conv_general_dilated | solution.py:45
  78.4 67.6 %psum.42 = f32[2,64]{1,0:T(2,128)S(1)} all-reduce(f32[2,64]{1,0:T(2,128)S(1)} %reduce_sum.59), channel_id=1, replica_groups=mesh['dp'=32,'rows'=4] {'dp','rows'}, use_global_device_ids=true, to_apply=%region_1.2 | all-reduce | flops 128 | bytes 1024 | tf_op jit(solution)/shard_map/psum | solution.py:66
  146.0 3.0 copy.71
  150.9 3.6 copy.72
  154.5 4.2 reshape.84
  158.8 6.2 %fusion.14 = f32[2,64,64]{2,1,0:T(8,128)S(1)} fusion(f32[6144,2,64]{0,2,1:T(8,128)} %reshape.84, f32[2,64]{1,0:T(2,128)S(1)} %broadcast_multiply_fusion.3), kind=kOutput, calls=%fused_computation.28 | convolution fusion | flops 604766208 | bytes 3179008 | tf_op jit(solution)/shard_map/pgi,pgj->gij/dot_general | solution.py:68
  165.0 5.6 fusion.11
  170.6 63.8 %psum.43 = f32[2,64,64]{2,1,0:T(8,128)S(1)} all-reduce(f32[2,64,64]{2,1,0:T(8,128)S(1)} %fusion.14), channel_id=1, replica_groups=mesh['dp'=32,'rows'=4] {'dp','rows'}, use_global_device_ids=true, to_apply=%region_2.3 | all-reduce | flops 8192 | bytes 65536 | tf_op jit(solution)/shard_map/psum | solution.py:69
  237.7 5.2 convolution_bitcast_fusion.1
  247.0 4.9 fusion.2
  254.3 130.2 %all-reduce.7.cloned.1.call-done = (f32[2,64,64]{2,1,0:T(8,128)}, f32[2,64]{1,0:T(2,128)}, f32[2,64,64]{1,2,0:T(8,128)}) async-done(((f32[2,64,64]{2,1,0:T(8,128)}, f32[2,64]{1,0:T(2,128)}, f32[2,64,64]{1,2,0:T(8,128)}), (f32[2,64,64]{2,1,0:T(8,128)}, f32[2,64]{1,0:T(2,128)}, f32[2,64,64]{1,2,0:T(8,128)})) %all-reduce.7.cloned.1.call-update) | async-done | bytes 66064 | tf_op jit(solution)/shard_map/psum | solution.py:82
  394.9 5.2 convolution_multiply_fusion
  400.2 3.1 fusion.3
  414.4 3.8 collective-permute-start.2
  435.0 3.6 reshape.107
  440.1 4.8 select_convert_fusion
  448.8 130.5 %all-reduce.5.cloned.1.call-done = f32[3,3,256,128]{3,2,1,0:T(8,128)} async-done(((f32[3,3,256,128]{3,2,1,0:T(8,128)}), f32[3,3,256,128]{3,2,1,0:T(8,128)}) %all-reduce.5.cloned.1.call-update) | async-done | bytes 1179664 | tf_op jit(solution)/shard_map/psum | solution.py:113
  (155 shorter events, 73.3 us)
Async XLA Ops:
  7.2 61.2 %copy-start = (bf16[3,3,256,128]{3,2,1,0:T(8,128)(2,1)S(1)}, bf16[3,3,256,128]{3,2,1,0:T(8,128)(2,1)}, u32[]{:S(2)}) copy-start(bf16[3,3,256,128]{3,2,1,0:T(8,128)(2,1)} %param.6) | copy-start | bytes 1769476
  7.2 10.4 %copy-start.13 = (bf16[6,8,128,128]{3,2,1,0:T(8,128)(2,1)S(1)}, bf16[6,8,128,128]{3,2,1,0:T(8,128)(2,1)}, u32[]{:S(2)}) copy-start(bf16[6,8,128,128]{3,2,1,0:T(8,128)(2,1)} %param.9) | copy-start | bytes 4718596
  7.2 377.3 %all-reduce.7.cloned.1.call-start = ((), (), s32[]{:S(2)}) async-start(), calls=%async_computation.1 | async-start | bytes 264192 | tf_op jit(solution)/shard_map/psum | solution.py:82
  9.3 19.8 %collective-permute-start.1 = (bf16[6,1,128,256]{3,2,1,0:T(8,128)(2,1)S(1)}, bf16[6,1,128,256]{3,2,1,0:T(8,128)(2,1)S(1)}, u32[]{:S(2)}, u32[]{:S(2)}) collective-permute-start(bf16[6,1,128,256]{3,2,1,0:T(8,128)(2,1)S(1)} %get-tuple-element.28), channel_id=1, source_target_pairs={{1,0},{2,1},{3,2},{5,4},{6,5},{7,6},{9,8},{10,9},{11,10},{13,12},{... | collective-permute-start | bytes 1179656 | tf_op jit(solution)/shard_map/ppermute | solution.py:23
  10.6 18.4 %collective-permute-start = (bf16[6,1,128,256]{3,2,1,0:T(8,128)(2,1)}, bf16[6,1,128,256]{3,2,1,0:T(8,128)(2,1)S(1)}, u32[]{:S(2)}, u32[]{:S(2)}) collective-permute-start(bf16[6,1,128,256]{3,2,1,0:T(8,128)(2,1)} %get-tuple-element.29), channel_id=1, source_target_pairs={{0,1},{1,2},{2,3},{4,5},{5,6},{6,7},{8,9},{9,10},{10,11},{12,13},{... | collective-permute-start | bytes 1179656 | tf_op jit(solution)/shard_map/ppermute | solution.py:20
  17.5 5.2 copy-start.14
  22.7 3.8 copy-start.20
  64.0 4.4 copy-start.21
  158.8 6.2 %copy-start.1 = (f32[6144,2,64]{0,2,1:T(8,128)S(1)}, f32[6144,2,64]{0,2,1:T(8,128)}, u32[]{:S(2)}) copy-start(f32[6144,2,64]{0,2,1:T(8,128)} %reshape.84) | copy-start | bytes 9437188
  165.0 69.7 %copy-start.17 = (f32[64,64]{1,0:T(8,128)S(1)}, f32[64,64]{1,0:T(8,128)}, u32[]{:S(2)}) copy-start(f32[64,64]{1,0:T(8,128)} %copy.73) | copy-start | bytes 49156
  244.6 2.3 copy-start.19
  246.9 332.3 %all-reduce.5.cloned.1.call-start = ((), (), s32[]{:S(2)}) async-start(), calls=%async_computation | async-start | bytes 2359296 | tf_op jit(solution)/shard_map/psum | solution.py:113
  384.5 7.9 %copy-start.15 = (f32[2,64,64]{2,1,0:T(8,128)S(1)}, f32[2,64,64]{2,1,0:T(8,128)}, u32[]{:S(2)}) copy-start(f32[2,64,64]{2,1,0:T(8,128)} %get-tuple-element.16) | copy-start | bytes 98308
  384.5 8.1 %copy-start.18 = (f32[2,64]{1,0:T(2,128)S(1)}, f32[2,64]{1,0:T(2,128)}, u32[]{:S(2)}) copy-start(f32[2,64]{1,0:T(2,128)} %get-tuple-element.17) | copy-start | bytes 1540
  394.9 5.2 copy-start.2
  400.2 3.1 copy-start.6
  404.3 2.3 copy-start.16
  404.3 2.3 copy-start.4
  412.4 10.0 %copy-start.11 = (bf16[6,8,128,256]{3,2,1,0:T(8,128)(2,1)S(1)}, bf16[6,8,128,256]{3,2,1,0:T(8,128)(2,1)}, u32[]{:S(2)}) copy-start(bf16[6,8,128,256]{3,2,1,0:T(8,128)(2,1)} %get-tuple-element.20) | copy-start | bytes 9437188
  414.4 17.2 %collective-permute-start.2 = (bf16[6,1,128,128]{3,2,0,1:T(8,128)(2,1)}, bf16[6,1,128,128]{3,2,0,1:T(8,128)(2,1)}, u32[]{:S(2)}, u32[]{:S(2)}) collective-permute-start(bf16[6,1,128,128]{3,2,0,1:T(8,128)(2,1)} %get-tuple-element.30), channel_id=1, source_target_pairs={{0,1},{1,2},{2,3},{4,5},{5,6},{6,7},{8,9},{9,10},{10,11},{12,13},{... | collective-permute-start | bytes 589832 | tf_op jit(solution)/shard_map/ppermute | solution.py:20
  418.2 13.4 %collective-permute-start.3 = (bf16[6,1,128,128]{3,2,0,1:T(8,128)(2,1)}, bf16[6,1,128,128]{3,2,0,1:T(8,128)(2,1)}, u32[]{:S(2)}, u32[]{:S(2)}) collective-permute-start(bf16[6,1,128,128]{3,2,0,1:T(8,128)(2,1)} %get-tuple-element.31), channel_id=1, source_target_pairs={{1,0},{2,1},{3,2},{5,4},{6,5},{7,6},{9,8},{10,9},{11,10},{13,12},{... | collective-permute-start | bytes 589832 | tf_op jit(solution)/shard_map/ppermute | solution.py:23
  423.5 2.1 copy-start.9
  426.6 2.1 copy-start.7
  429.7 2.0 copy-start.12
  (5 other events, 8.7 us)
Sparse Core Ops, SparseCore 0:
  247.0 137.4 all-reduce.6
  431.7 147.4 all-reduce.4
where the time goes:
time: 598 us; the launch traced here: 589 us
  waiting for transfers between devices  261 us (44%)
  blocking collectives  131 us (22%)
  matrix products  76.9 us (13%)
  local copies, waits for them, and re-layouts  74 us (12%)
  other arithmetic  19.3 us (3%)
  between operations  15.1 us (3%)
  starting transfers between devices  11.1 us (2%)
    psum x1, waiting for transfers between devices, body(): summed = lax.psum(kernel_term, ('dp', 'rows'))  130 us
    psum x1, waiting for transfers between devices, body(): lax.psum((local_up, local_color, local_whiten), ('dp', 'rows'))  130 us
    psum x1, blocking collectives, body(): average = lax.psum(jnp.sum(raw_cols, axis=0), ('dp', 'rows')) / total_pix  67.6 us
    psum x1, blocking collectives, body(): covariance = lax.psum(local_cov, ('dp', 'rows')) / total_pix  63.8 us
    conv_general_dilated x7, local copies, waits for them, and re-layouts, filter_valid(): lax.conv_general_dilated(source, weights, (1, 1), 'VALID', dimension_numb...  21.9 us
    conv_general_dilated x2, matrix products, filter_valid(): lax.conv_general_dilated(source, weights, (1, 1), 'VALID', dimension_numb...  14.8 us
    dot_general x40, matrix products, batched(): return jnp.einsum('gij,gjk->gik', left, right, precision=PRECISE)  14.3 us
    unnamed x54, local copies, waits for them, and re-layouts  13.9 us
  transfers between devices with their start and end apart: 6, of which 2 were waited for; matrix products, arithmetic and copies ran while one was open for 8% of the time, Pallas kernels for 0%

commit v1 on v0

v1 whole, which is shorter than its diff:
```python
import functools
import math

import jax
import jax.numpy as jnp
from jax import lax
from jax.experimental import pallas as pl
from jax.experimental.pallas import tpu as pltpu
from jax.sharding import PartitionSpec as P

NS_ITERS = 5
EPSILON = 1e-05
PRECISE = lax.Precision.HIGHEST
BF16 = jnp.bfloat16
F32 = jnp.float32
MESH = pl.DeviceIdType.MESH

IMGS, BAND, WID, CIN, COUT, GS = 6, 8, 128, 256, 128, 64
RING = 4
OCT = 8
PIX = IMGS * BAND * WID
ONE_ROW = COUT * 3


def exact(left, right, dims=((1,), (0,))):
    return lax.dot_general(
        left, right, (dims, ((), ())), precision=PRECISE, preferred_element_type=F32
    )


def fast(left, right):
    return jnp.dot(left, right, preferred_element_type=F32)


def from_left(block):
    place = lax.broadcasted_iota(jnp.int32, block.shape, 0) % WID
    return jnp.where(place == 0, 0.0, pltpu.roll(block, 1, 0))


def from_right(block):
    place = lax.broadcasted_iota(jnp.int32, block.shape, 0) % WID
    return jnp.where(place == WID - 1, 0.0, pltpu.roll(block, block.shape[0] - 1, 0))


def pack(full):
    lane = lax.broadcasted_iota(jnp.int32, (GS, full.shape[1]), 1) % COUT
    return jnp.where(lane < GS, full[:GS], full[GS:])


def merged(buf, count, pixels, spare, place):
    rows = buf[0, 0:8]
    mean = buf[0, 8:16]
    for slot in range(1, count):
        rows = rows + buf[slot, 0:8]
        mean = mean + buf[slot, 8:16]
    mean = mean * (1.0 / count)
    index = lax.broadcasted_iota(jnp.int32, mean.shape, 0)
    apart = jnp.zeros_like(mean)
    for slot in range(count):
        apart = jnp.where(index == slot, buf[slot, 8:16] - mean, apart)
    between = pack(exact(apart[:, :COUT], apart, ((0,), (0,)))) * float(pixels)
    for slot in range(OCT):
        spare[slot] = between[slot * 8 : slot * 8 + 8]
    return rows + spare[place], mean


def upper(top):
    lane = lax.broadcasted_iota(jnp.int32, top.shape, 1)
    return jnp.concatenate([top, jnp.where(lane < GS, 0.0, pltpu.roll(top, GS, 1))], axis=0)


def diag_pair(first, second):
    zero = jnp.zeros((GS, GS), F32)
    return jnp.concatenate(
        [
            jnp.concatenate([first, zero], axis=1),
            jnp.concatenate([zero, second], axis=1),
        ],
        axis=0,
    )


def whiten_terms(packed, colors, total_pix):
    row = lax.broadcasted_iota(jnp.int32, (GS, GS), 0)
    col = lax.broadcasted_iota(jnp.int32, (GS, GS), 1)
    eye = jnp.where(row == col, 1.0, 0.0).astype(F32)
    cross = packed[:, COUT:].T
    tops, fulls, traces, crosses = [], [], [], []
    for group in range(2):
        sigma = packed[:, group * GS : (group + 1) * GS] * (1.0 / total_pix) + EPSILON * eye
        trace = jnp.sum(jnp.sum(sigma * eye, axis=1, keepdims=True), axis=0, keepdims=True)
        along = cross[group * GS : (group + 1) * GS]
        grad = exact(colors[group].T, along)
        tops.append(jnp.concatenate([sigma / trace, grad], axis=1))
        fulls.append(upper(tops[-1]))
        traces.append(trace)
        crosses.append(along)
    wide_eye = jnp.concatenate([eye, jnp.zeros((GS, GS), F32)], axis=1)
    states = [1.5 * wide_eye - 0.5 * top for top in tops]
    for _ in range(NS_ITERS - 1):
        squares = [exact(state, upper(state)) for state in states]
        by_normed = [exact(state, full) for state, full in zip(states, fulls)]
        cubes = [exact(square, upper(term)) for square, term in zip(squares, by_normed)]
        states = [1.5 * state - 0.5 * cube for state, cube in zip(states, cubes)]
    found = []
    for group in range(2):
        trace = traces[group]
        root = lax.rsqrt(trace)
        estimate, slope = states[group][:, :GS], states[group][:, GS:]
        normed, grad = tops[group][:, :GS], tops[group][:, GS:]
        scalar = slope * normed + 0.5 * grad * estimate
        scalar = jnp.sum(jnp.sum(scalar, axis=1, keepdims=True), axis=0, keepdims=True)
        sigma_grad = (slope - eye * scalar) * (root / trace)
        both = (sigma_grad + sigma_grad.T) * (1.0 / total_pix)
        whitener = estimate * root
        colored_by = exact(colors[group], whitener)
        color_sum = exact(crosses[group], whitener, ((1,), (1,)))
        found.append((colored_by, both, color_sum))
    return found


def block_kernel(
    total_pix,
    images,
    kernel,
    colors,
    offset,
    upstream,
    colored,
    grad_images,
    kernel_sum,
    color_grad,
    img,
    x3,
    pre,
    wf,
    wb,
    imgt,
    pg3,
    pg_halo,
    col_buf,
    gi_buf,
    sums,
    moments,
    rhi,
    rlo,
    consts,
    stat_src,
    stat_a,
    stat_y,
    stat_z,
    stat_all,
    spare,
    gk,
    rx0,
    rx1,
    acc1,
    rx2,
    rx3,
    ag2,
    ag1,
    load_sem,
    weight_sem,
    store_sem,
    halo_send,
    halo_recv,
    oct_send,
    oct_recv,
    line_send,
    line_recv,
    back_send,
    back_recv,
    pg_send,
    pg_recv,
    gk_core_send,
    gk_core_recv,
    gk_send,
    gk_recv,
):
    dp = lax.axis_index("dp")
    y = lax.axis_index("rows")
    x = dp // (RING * 2)
    z = (dp // 2) % RING
    core = dp % 2
    octet = x * 2 + core

    def oct_device(index):
        return (((index // 2) * RING + z) * 2 + index % 2, y)

    def along(axis, index):
        if axis == "x":
            return ((index * RING + z) * 2 + core, y)
        if axis == "y":
            return (dp, index)
        return ((x * RING + index) * 2 + core, y)

    spot = {"x": x, "y": y, "z": z}

    loads = [
        pltpu.make_async_copy(images.at[b], img.at[b, pl.ds(1, BAND)], load_sem.at[b])
        for b in range(IMGS)
    ]
    up_load = pltpu.make_async_copy(
        upstream, x3.at[:, :, :, pl.ds(2 * COUT, COUT)], load_sem.at[IMGS]
    )
    weight_loads = [
        pltpu.make_async_copy(
            kernel.at[a, c],
            wf.at[pl.ds(a * CIN, CIN), pl.ds(c * COUT, COUT)],
            weight_sem.at[a * 3 + c],
        )
        for a in range(3)
        for c in range(3)
    ]
    for copy in weight_loads:
        copy.start()
    for copy in loads:
        copy.start()
    up_load.start()

    barrier = pltpu.get_barrier_semaphore()
    for k in range(1, OCT):
        pl.semaphore_signal(
            barrier, inc=1, device_id=oct_device((octet + k) % OCT), device_id_type=MESH
        )
    for axis in ("y", "z"):
        for k in range(1, RING):
            pl.semaphore_signal(
                barrier,
                inc=1,
                device_id=along(axis, (spot[axis] + k) % RING),
                device_id_type=MESH,
            )
    pl.semaphore_wait(barrier, OCT - 1 + 2 * (RING - 1))

    halo_up = pltpu.make_async_remote_copy(
        src_ref=images.at[:, 0],
        dst_ref=img.at[:, BAND + 1],
        send_sem=halo_send.at[0],
        recv_sem=halo_recv.at[0],
        device_id=along("y", (y + RING - 1) % RING),
        device_id_type=MESH,
    )
    halo_down = pltpu.make_async_remote_copy(
        src_ref=images.at[:, BAND - 1],
        dst_ref=img.at[:, 0],
        send_sem=halo_send.at[1],
        recv_sem=halo_recv.at[1],
        device_id=along("y", (y + 1) % RING),
        device_id_type=MESH,
    )

    @pl.when(y > 0)
    def _():
        halo_up.start()

    @pl.when(y < RING - 1)
    def _():
        halo_down.start()

    @pl.when(y == 0)
    def _():
        img[:, 0] = jnp.zeros((IMGS, WID, CIN), BF16)
        pg3[:, 0] = jnp.zeros((IMGS, WID, ONE_ROW), BF16)

    @pl.when(y == RING - 1)
    def _():
        img[:, BAND + 1] = jnp.zeros((IMGS, WID, CIN), BF16)
        pg3[:, BAND + 1] = jnp.zeros((IMGS, WID, ONE_ROW), BF16)

    for copy in weight_loads:
        copy.wait()
    for copy in loads:
        copy.wait()

    sums[...] = jnp.zeros_like(sums)

    def conv(lhs):
        out = fast(lhs, wf[...])
        return (
            from_left(out[:, :COUT])
            + out[:, COUT : 2 * COUT]
            + from_right(out[:, 2 * COUT :])
        )

    def count_in(block):
        part = block.reshape(-1, 8, COUT).sum(axis=0)
        sums[:, :COUT] = sums[:, :COUT] + part

    inner = BAND - 2

    @pl.loop(0, IMGS)
    def _(b):
        lhs = jnp.concatenate(
            [img[b, pl.ds(1 + a, inner)].reshape(inner * WID, CIN) for a in range(3)], axis=1
        )
        block = conv(lhs)
        count_in(block)
        pre[b, pl.ds(1, inner)] = block.reshape(inner, WID, COUT)

    for a in range(3):
        for c in range(3):
            tap = wf[a * CIN : (a + 1) * CIN, c * COUT : (c + 1) * COUT]
            wb[a * ONE_ROW + c * COUT : a * ONE_ROW + (c + 1) * COUT, :] = tap.T
    up_load.wait()

    @pl.loop(0, IMGS)
    def _(b):
        for h in range(BAND):
            imgt[b, :, h * WID : (h + 1) * WID] = img[b, h + 1].T
        ups = x3[b, :, :, 2 * COUT :].reshape(-1, 8, COUT).astype(F32).sum(axis=0)
        sums[:, COUT:] = sums[:, COUT:] + ups

    @pl.when(y < RING - 1)
    def _():
        halo_up.wait_recv()

    @pl.when(y > 0)
    def _():
        halo_down.wait_recv()

    @pl.loop(0, IMGS)
    def _(b):
        lhs = jnp.concatenate(
            [
                jnp.concatenate([img[b, a], img[b, BAND - 1 + a]], axis=0)
                for a in range(3)
            ],
            axis=1,
        )
        block = conv(lhs)
        count_in(block)
        pre[b, 0] = block[:WID]
        pre[b, BAND - 1] = block[WID:]

    own = jnp.sum(sums[...], axis=0, keepdims=True) * (1.0 / PIX)
    own_mean = own[:, :COUT]
    moments[...] = jnp.zeros_like(moments)

    @pl.loop(0, IMGS)
    def _(b):
        apart = pre[b].reshape(BAND * WID, COUT) - own_mean
        high = apart.astype(BF16)
        low = (apart - high.astype(F32)).astype(BF16)
        x3[b, :, :, :COUT] = low.reshape(BAND, WID, COUT)
        x3[b, :, :, COUT : 2 * COUT] = high.reshape(BAND, WID, COUT)
        ups = x3[b, :, :, 2 * COUT :].reshape(BAND * WID, COUT)
        moments[...] = moments[...] + fast(high.T, jnp.concatenate([high, ups], axis=1))

    packed = pack(moments[...])
    wide_own = jnp.broadcast_to(own, (8, 2 * COUT))
    for slot in range(OCT):
        stat_src[slot, 0:8] = packed[slot * 8 : slot * 8 + 8]
        stat_src[slot, 8:16] = wide_own

    copies = []
    for k in range(1, OCT):
        target = (octet + k) % OCT
        copies.append(
            pltpu.make_async_remote_copy(
                src_ref=stat_src.at[target],
                dst_ref=stat_a.at[octet],
                send_sem=oct_send.at[k - 1],
                recv_sem=oct_recv.at[k - 1],
                device_id=oct_device(target),
                device_id_type=MESH,
            )
        )
    for copy in copies:
        copy.start()
    stat_a[octet] = stat_src[octet]
    for copy in copies:
        copy.wait()
    rows, mean = merged(stat_a, OCT, PIX, spare, octet)
    pixels = PIX * OCT
    for number, (axis, buf) in enumerate((("y", stat_y), ("z", stat_z))):
        me = spot[axis]
        buf[me, 0:8] = rows
        buf[me, 8:16] = mean
        copies = [
            pltpu.make_async_remote_copy(
                src_ref=buf.at[me],
                dst_ref=buf.at[me],
                send_sem=line_send.at[number, k - 1],
                recv_sem=line_recv.at[number, k - 1],
                device_id=along(axis, (me + k) % RING),
                device_id_type=MESH,
            )
            for k in range(1, RING)
        ]
        for copy in copies:
            copy.start()
        for copy in copies:
            copy.wait()
        rows, mean = merged(buf, RING, pixels, spare, octet)
        pixels = pixels * RING
    stat_all[octet, 0:8] = rows
    stat_all[octet, 8:16] = mean
    copies = [
        pltpu.make_async_remote_copy(
            src_ref=stat_all.at[octet],
            dst_ref=stat_all.at[octet],
            send_sem=back_send.at[k - 1],
            recv_sem=back_recv.at[k - 1],
            device_id=oct_device((octet + k) % OCT),
            device_id_type=MESH,
        )
        for k in range(1, OCT)
    ]
    for copy in copies:
        copy.start()
    for copy in copies:
        copy.wait()
    packed = jnp.concatenate([stat_all[slot, 0:8] for slot in range(OCT)], axis=0)
    all_mean = stat_all[0, 8:16]

    (t0, b0, s0), (t1, b1, s1) = whiten_terms(packed, colors, total_pix)
    color_grad[0] = s0 * (1.0 / math.sqrt(total_pix))
    color_grad[1] = s1 * (1.0 / math.sqrt(total_pix))
    by_x = jnp.concatenate([diag_pair(t0.T, t1.T), diag_pair(b0, b1)], axis=1)
    by_up = jnp.concatenate([jnp.zeros((COUT, COUT), F32), diag_pair(t0, t1)], axis=1)
    x_high, up_high = by_x.astype(BF16), by_up.astype(BF16)
    rhi[0:COUT] = x_high
    rhi[COUT : 2 * COUT] = x_high
    rhi[2 * COUT :] = up_high
    rlo[0:COUT] = (by_x - x_high.astype(F32)).astype(BF16)
    rlo[COUT:] = (by_up - up_high.astype(F32)).astype(BF16)
    shift = wide_own[:, :COUT] - all_mean[:, :COUT]
    level = exact(shift, by_x) - exact(all_mean[:, COUT:], by_up)
    consts[:, :COUT] = level[:, :COUT] + offset[...]
    consts[:, COUT:] = level[:, COUT:]

    def spread(block):
        return jnp.concatenate(
            [from_right(block).astype(BF16), block.astype(BF16), from_left(block).astype(BF16)],
            axis=1,
        )

    def finish(lhs):
        out = fast(lhs, rhi[...]) + fast(lhs[:, COUT:], rlo[...]) + consts[0:1, :]
        return out[:, :COUT].astype(BF16), spread(out[:, COUT:])

    @pl.loop(0, IMGS)
    def _(b):
        lhs = jnp.concatenate([x3[b, 0], x3[b, BAND - 1]], axis=0)
        shown, grads = finish(lhs)
        col_buf[b, 0] = shown[:WID]
        col_buf[b, BAND - 1] = shown[WID:]
        pg3[b, 1] = grads[:WID]
        pg3[b, BAND] = grads[WID:]

    pg_up = pltpu.make_async_remote_copy(
        src_ref=pg3.at[:, 1, :, pl.ds(COUT, COUT)],
        dst_ref=pg_halo.at[1],
        send_sem=pg_send.at[0],
        recv_sem=pg_recv.at[0],
        device_id=along("y", (y + RING - 1) % RING),
        device_id_type=MESH,
    )
    pg_down = pltpu.make_async_remote_copy(
        src_ref=pg3.at[:, BAND, :, pl.ds(COUT, COUT)],
        dst_ref=pg_halo.at[0],
        send_sem=pg_send.at[1],
        recv_sem=pg_recv.at[1],
        device_id=along("y", (y + 1) % RING),
        device_id_type=MESH,
    )

    @pl.when(y > 0)
    def _():
        pg_up.start()

    @pl.when(y < RING - 1)
    def _():
        pg_down.start()

    @pl.loop(0, IMGS)
    def _(b):
        shown, grads = finish(x3[b, pl.ds(1, inner)].reshape(inner * WID, 3 * COUT))
        col_buf[b, pl.ds(1, inner)] = shown.reshape(inner, WID, COUT)
        pg3[b, pl.ds(2, inner)] = grads.reshape(inner, WID, ONE_ROW)

    col_store = pltpu.make_async_copy(col_buf, colored, store_sem.at[IMGS])
    col_store.start()

    orders = (("x", "y", "z"), ("y", "z", "x"), ("z", "x", "y"))

    def weight_part(a):
        gk[a] = jnp.zeros((CIN, ONE_ROW), F32)

        @pl.loop(0, IMGS)
        def _(b):
            rhs = pg3[b, pl.ds(2 - a, BAND)].reshape(BAND * WID, ONE_ROW)
            gk[a] = gk[a] + fast(imgt[b], rhs)

    core_rows = CIN // 2
    ring_rows = core_rows // RING
    last_rows = ring_rows // RING
    other_core = (dp + 1 - 2 * core, y)

    def rows_at(start, size):
        return pl.ds(pl.multiple_of(start, size), size)

    def ring_copies(part, stage, src, dst):
        axis = orders[part][(0, 1, 2, 1, 0)[stage]]
        me = spot[axis]
        return [
            pltpu.make_async_remote_copy(
                src_ref=src((me + k) % RING),
                dst_ref=dst(k),
                send_sem=gk_send.at[part, stage, k - 1],
                recv_sem=gk_recv.at[part, stage, k - 1],
                device_id=along(axis, (me + k) % RING),
                device_id_type=MESH,
            )
            for k in range(1, RING)
        ]

    flying = {}

    def start(part, copies):
        for copy in copies:
            copy.start()
        flying[part] = copies

    def settle(part):
        for copy in flying[part]:
            copy.wait()

    def step(part, stage):
        first, second, third = (spot[axis] for axis in orders[part])
        mine = core * core_rows
        if stage > 0:
            settle(part)
        if stage == 0:
            start(
                part,
                [
                    pltpu.make_async_remote_copy(
                        src_ref=gk.at[part, rows_at((1 - core) * core_rows, core_rows)],
                        dst_ref=rx0.at[part],
                        send_sem=gk_core_send.at[part, 0],
                        recv_sem=gk_core_recv.at[part, 0],
                        device_id=other_core,
                        device_id_type=MESH,
                    )
                ],
            )
        elif stage == 1:
            here = rows_at(mine, core_rows)
            gk[part, here] = gk[part, here] + rx0[part]
            start(
                part,
                ring_copies(
                    part,
                    0,
                    lambda piece: gk.at[part, rows_at(mine + piece * ring_rows, ring_rows)],
                    lambda k: rx1.at[part, k - 1],
                ),
            )
        elif stage == 2:
            held = gk[part, rows_at(mine + first * ring_rows, ring_rows)]
            acc1[part] = held + rx1[part, 0] + rx1[part, 1] + rx1[part, 2]
            start(
                part,
                ring_copies(
                    part,
                    1,
                    lambda piece: acc1.at[part, rows_at(piece * last_rows, last_rows)],
                    lambda k: rx2.at[part, k - 1],
                ),
            )
        elif stage == 3:
            held = acc1[part, rows_at(second * last_rows, last_rows)]
            rx3[part, third] = held + rx2[part, 0] + rx2[part, 1] + rx2[part, 2]
            start(
                part,
                ring_copies(
                    part, 2, lambda piece: rx3.at[part, third], lambda k: rx3.at[part, third]
                ),
            )
        elif stage == 4:
            here = rows_at(second * last_rows, last_rows)
            ag2[part, here] = (rx3[part, 0] + rx3[part, 1]) + (rx3[part, 2] + rx3[part, 3])
            start(
                part,
                ring_copies(
                    part, 3, lambda piece: ag2.at[part, here], lambda k: ag2.at[part, here]
                ),
            )
        elif stage == 5:
            here = rows_at(mine + first * ring_rows, ring_rows)
            ag1[part, here] = ag2[part].astype(BF16)
            start(
                part,
                ring_copies(
                    part, 4, lambda piece: ag1.at[part, here], lambda k: ag1.at[part, here]
                ),
            )
        elif stage == 6:
            here = rows_at(mine, core_rows)
            start(
                part,
                [
                    pltpu.make_async_remote_copy(
                        src_ref=ag1.at[part, here],
                        dst_ref=ag1.at[part, here],
                        send_sem=gk_core_send.at[part, 1],
                        recv_sem=gk_core_recv.at[part, 1],
                        device_id=other_core,
                        device_id_type=MESH,
                    )
                ],
            )

    gi_stores = [
        pltpu.make_async_copy(gi_buf.at[b], grad_images.at[b], store_sem.at[b])
        for b in range(IMGS)
    ]

    def image_grad(b):
        half = BAND // 2

        @pl.loop(0, 2)
        def _(part):
            lhs = jnp.concatenate(
                [
                    pg3[b, pl.ds(part * half + 2 - a, half)].reshape(half * WID, ONE_ROW)
                    for a in range(3)
                ],
                axis=1,
            )
            out = fast(lhs, wb[...]).astype(BF16)
            gi_buf[b, pl.ds(part * half, half)] = out.reshape(half, WID, CIN)

        gi_stores[b].start()

    weight_part(1)
    step(1, 0)

    @pl.when(y < RING - 1)
    def _():
        pg_up.wait_recv()

        @pl.loop(0, IMGS)
        def _(b):
            pg3[b, BAND + 1] = spread(pg_halo[1, b].astype(F32))

    @pl.when(y > 0)
    def _():
        pg_down.wait_recv()

        @pl.loop(0, IMGS)
        def _(b):
            pg3[b, 0] = spread(pg_halo[0, b].astype(F32))

    weight_part(0)
    step(0, 0)
    step(1, 1)
    weight_part(2)
    step(2, 0)
    step(0, 1)
    step(1, 2)
    image_grad(0)
    step(2, 1)
    step(0, 2)
    step(1, 3)
    image_grad(1)
    step(2, 2)
    step(0, 3)
    step(1, 4)
    image_grad(2)
    step(2, 3)
    step(0, 4)
    step(1, 5)
    image_grad(3)
    step(2, 4)
    step(0, 5)
    step(1, 6)
    image_grad(4)
    step(2, 5)
    step(0, 6)
    image_grad(5)
    step(2, 6)
    for part in (1, 0, 2):
        settle(part)
    last = pltpu.make_async_copy(ag1, kernel_sum, store_sem.at[IMGS + 1])
    last.start()

    @pl.when(y > 0)
    def _():
        halo_up.wait_send()
        pg_up.wait_send()

    @pl.when(y < RING - 1)
    def _():
        halo_down.wait_send()
        pg_down.wait_send()

    col_store.wait()
    for copy in gi_stores:
        copy.wait()
    last.wait()


def body(images, kernel, colors, offset, upstream):
    total_pix = PIX * lax.axis_size("dp") * lax.axis_size("rows")
    anywhere = pl.BlockSpec(memory_space=pl.ANY)
    local = pl.BlockSpec(memory_space=pltpu.VMEM)
    dma = pltpu.SemaphoreType.DMA
    colored, grad_images, kernel_sum, color_grad = pl.pallas_call(
        functools.partial(block_kernel, total_pix),
        out_shape=(
            jax.ShapeDtypeStruct((IMGS, BAND, WID, COUT), BF16),
            jax.ShapeDtypeStruct((IMGS, BAND, WID, CIN), BF16),
            jax.ShapeDtypeStruct((3, CIN, ONE_ROW), BF16),
            jax.ShapeDtypeStruct((2, GS, GS), F32),
        ),
        in_specs=[anywhere, anywhere, local, local, anywhere],
        out_specs=(anywhere, anywhere, anywhere, local),
        scratch_shapes=[
            pltpu.VMEM((IMGS, BAND + 2, WID, CIN), BF16),
            pltpu.VMEM((IMGS, BAND, WID, 3 * COUT), BF16),
            pltpu.VMEM((IMGS, BAND, WID, COUT), F32),
            pltpu.VMEM((3 * CIN, ONE_ROW), BF16),
            pltpu.VMEM((3 * ONE_ROW, CIN), BF16),
            pltpu.VMEM((IMGS, CIN, BAND * WID), BF16),
            pltpu.VMEM((IMGS, BAND + 2, WID, ONE_ROW), BF16),
            pltpu.VMEM((2, IMGS, WID, COUT), BF16),
            pltpu.VMEM((IMGS, BAND, WID, COUT), BF16),
            pltpu.VMEM((IMGS, BAND, WID, CIN), BF16),
            pltpu.VMEM((8, 2 * COUT), F32),
            pltpu.VMEM((COUT, 2 * COUT), F32),
            pltpu.VMEM((3 * COUT, 2 * COUT), BF16),
            pltpu.VMEM((2 * COUT, 2 * COUT), BF16),
            pltpu.VMEM((8, 2 * COUT), F32),
            pltpu.VMEM((OCT, 16, 2 * COUT), F32),
            pltpu.VMEM((OCT, 16, 2 * COUT), F32),
            pltpu.VMEM((RING, 16, 2 * COUT), F32),
            pltpu.VMEM((RING, 16, 2 * COUT), F32),
            pltpu.VMEM((OCT, 16, 2 * COUT), F32),
            pltpu.VMEM((OCT, 8, 2 * COUT), F32),
            pltpu.VMEM((3, CIN, ONE_ROW), F32),
            pltpu.VMEM((3, CIN // 2, ONE_ROW), F32),
            pltpu.VMEM((3, RING - 1, CIN // 8, ONE_ROW), F32),
            pltpu.VMEM((3, CIN // 8, ONE_ROW), F32),
            pltpu.VMEM((3, RING - 1, CIN // 32, ONE_ROW), F32),
            pltpu.VMEM((3, RING, CIN // 32, ONE_ROW), F32),
            pltpu.VMEM((3, CIN // 8, ONE_ROW), F32),
            pltpu.VMEM((3, CIN, ONE_ROW), BF16),
            dma((IMGS + 1,)),
            dma((9,)),
            dma((IMGS + 2,)),
            dma((2,)),
            dma((2,)),
            dma((OCT - 1,)),
            dma((OCT - 1,)),
            dma((2, RING - 1)),
            dma((2, RING - 1)),
            dma((OCT - 1,)),
            dma((OCT - 1,)),
            dma((2,)),
            dma((2,)),
            dma((3, 2)),
            dma((3, 2)),
            dma((3, 5, RING - 1)),
            dma((3, 5, RING - 1)),
        ],
        compiler_params=pltpu.CompilerParams(
            collective_id=0, has_side_effects=True, vmem_limit_bytes=56 * 1024 * 1024
        ),
    )(images, kernel, colors, offset.reshape(1, COUT), upstream)
    scaling = 1.0 / math.sqrt(total_pix)
    taps = kernel_sum.reshape(3, CIN, 3, COUT).transpose(0, 2, 1, 3).astype(F32) * scaling
    return colored, grad_images, taps, color_grad


def solution(mesh):
    placed = (P("dp", "rows", None, None), P(), P(), P(), P("dp", "rows", None, None))
    return jax.shard_map(
        body,
        mesh=mesh,
        in_specs=placed,
        out_specs=(P("dp", "rows", None, None), P("dp", "rows", None, None), P(), P()),
        check_vma=False,
    )
```

time: 598 us -> 92.2 us (0.15); the launches traced: 589 us -> 92 us
  waiting for transfers between devices: 261 us -> 0 us
  blocking collectives: 131 us -> 0 us
  Pallas kernels: 0 us -> 83.3 us
  matrix products: 76.9 us -> 0 us
  local copies, waits for them, and re-layouts: 74 us -> 6.93 us
  other arithmetic: 19.3 us -> 1.17 us
  between operations: 15.1 us -> 0.65 us
  starting transfers between devices: 11.1 us -> 0 us
    psum x2 -> x0, waiting for transfers between devices: 261 us -> none  [the longest x1 130 us: body(): summed = lax.psum(kernel_term, ('dp', 'rows'))]
    psum x2 -> x0, blocking collectives: 131 us -> none  [the longest x1 67.6 us: body(): average = lax.psum(jnp.sum(raw_cols, axis=0), ('dp', 'rows')) / total_pix]
    pallas_call x0 -> x1, Pallas kernels: none -> 83.3 us  [body(): pl.pallas_call(functools.partial(block_kernel, total_pix), out_shape=(jax...]
    dot_general x59 -> x0, matrix products: 62.2 us -> none  [the longest x40 14.3 us: batched(): return jnp.einsum('gij,gjk->gik', left, right, precision=PRECISE)]
    conv_general_dilated x7 -> x0, local copies, waits for them, and re-layouts: 21.9 us -> none  [filter_valid(): lax.conv_general_dilated(source, weights, (1, 1), 'VALID', dimension_numb...]
    slice x3 -> x0, local copies, waits for them, and re-layouts: 17.9 us -> none  [the longest x1 13.9 us: body(): padded[:, row_off:row_off + band_rows, col_off:col_off + width_n, :]]
    conv_general_dilated x2 -> x0, matrix products: 14.8 us -> none  [filter_valid(): lax.conv_general_dilated(source, weights, (1, 1), 'VALID', dimension_numb...]
    ppermute x4 -> x0, starting transfers between devices: 11.1 us -> none  [the longest x2 8.5 us: with_halo(): lax.ppermute(lax.slice_in_dim(block, block.shape[dim] - width, None, axis...]
  transfers between devices with their start and end apart: 6 -> 0, of which waited for: 2 -> 0; matrix products, arithmetic and copies ran while one was open for 8% -> 0% of each run, Pallas kernels for 0% -> 0%
where the time goes in v1:
time: 92.2 us; the launch traced here: 92 us
  Pallas kernels  83.3 us (90%)
  local copies, waits for them, and re-layouts  6.93 us (8%)
  other arithmetic  1.17 us (1%)
    pallas_call x1, Pallas kernels, body(): pl.pallas_call(functools.partial(block_kernel, total_pix), out_shape=(jax...  83.3 us
    unnamed x8, local copies, waits for them, and re-layouts  6.56 us

profile of v1, /device:TPU:1, one launch (start us, length us, event | category | flops | bytes accessed | tf_op | source)
XLA Modules:
  0.0 92.0 jit_solution(10294691781490020446)
XLA Ops:
  0.6 83.3 %shard_map.84 = (bf16[6,8,128,128]{3,2,1,0:T(8,128)(2,1)}, bf16[6,8,128,256]{3,2,1,0:T(8,128)(2,1)}, bf16[3,256,384]{2,1,0:T(8,128)(2,1)}, f32[2,64,64]{2,1,0:T(8,128)}) custom-call(bf16[6,8,128,256]{3,2,1,0:T(8,128)(2,1)} %images.1, bf16[3,3,256,128]{3,2,1,0:T(8,128)(2,1)} %kernel.1, f32[2,64,64]{2,1,0:T(8,128)} %colors.1, f32[1,128]{1,0:T(1,128)} %bitcast.5, ...), custom_call_target="tpu_custom_call" | custom-call | tf_op jit(solution)/shard_map/pallas_call | solution.py:711
  83.9 1.2 %convert_multiply_fusion = f32[3,256,384]{2,1,0:T(8,128)S(1)} fusion(bf16[3,256,384]{2,1,0:T(8,128)(2,1)} %get-tuple-element.10), kind=kLoop, calls=%fused_computation | loop fusion | flops 589824 | bytes 1769472 | tf_op jit(solution)/shard_map/mul | solution.py:774
  85.1 0.4 copy.10
  85.5 1.4 %copy.11 = f32[3,3,256,128]{3,2,1,0:T(8,128)} copy(f32[3,3,256,128]{2,3,1,0:T(8,128)S(1)} %bitcast.4) | data formatting | bytes 2359296
  86.8 0.0 copy-start
  86.8 2.9 %copy.15 = bf16[6,8,128,128]{3,2,1,0:T(8,128)(2,1)} copy(bf16[6,8,128,128]{3,2,1,0:T(8,128)(2,1)} %get-tuple-element.20) | data formatting | bytes 3145728
  89.7 0.0 copy-done
  89.7 0.0 copy-start.1
  89.7 1.7 %copy.16 = bf16[6,8,128,256]{3,2,1,0:T(8,128)(2,1)} copy(bf16[6,8,128,256]{3,2,1,0:T(8,128)(2,1)S(1)} %copy-done) | data formatting | bytes 6291456
  91.4 0.0 copy-done.1
  91.4 0.6 copy.17
Async XLA Ops:
  86.8 2.9 %copy-start = (bf16[6,8,128,256]{3,2,1,0:T(8,128)(2,1)S(1)}, bf16[6,8,128,256]{3,2,1,0:T(8,128)(2,1)}, u32[]{:S(2)}) copy-start(bf16[6,8,128,256]{3,2,1,0:T(8,128)(2,1)} %get-tuple-element.21) | copy-start | bytes 9437188
  89.7 1.7 %copy-start.1 = (f32[2,64,64]{2,1,0:T(8,128)S(1)}, f32[2,64,64]{2,1,0:T(8,128)}, u32[]{:S(2)}) copy-start(f32[2,64,64]{2,1,0:T(8,128)} %get-tuple-element.23) | copy-start | bytes 98308

commit v2 on v1

v2 whole, which is shorter than its diff:
```python
import functools
import math

import jax
import jax.numpy as jnp
from jax import lax
from jax.experimental import pallas as pl
from jax.experimental.pallas import tpu as pltpu
from jax.sharding import PartitionSpec as P

NS_ITERS = 5
EPSILON = 1e-05
PRECISE = lax.Precision.HIGHEST
BF16 = jnp.bfloat16
F32 = jnp.float32
MESH = pl.DeviceIdType.MESH

IMGS, BAND, WID, CIN, COUT, GS = 6, 8, 128, 256, 128, 64
RING = 4
OCT = 8
PLANE = 16
PIX = IMGS * BAND * WID
ONE_ROW = COUT * 3


def exact(left, right, dims=((1,), (0,))):
    return lax.dot_general(
        left, right, (dims, ((), ())), precision=PRECISE, preferred_element_type=F32
    )


def fast(left, right):
    return jnp.dot(left, right, preferred_element_type=F32)


def from_left(block):
    place = lax.broadcasted_iota(jnp.int32, block.shape, 0) % WID
    return jnp.where(place == 0, 0.0, pltpu.roll(block, 1, 0))


def from_right(block):
    place = lax.broadcasted_iota(jnp.int32, block.shape, 0) % WID
    return jnp.where(place == WID - 1, 0.0, pltpu.roll(block, block.shape[0] - 1, 0))


def pack(full):
    lane = lax.broadcasted_iota(jnp.int32, (GS, full.shape[1]), 1) % COUT
    return jnp.where(lane < GS, full[:GS], full[GS:])


def upper(top):
    lane = lax.broadcasted_iota(jnp.int32, top.shape, 1)
    return jnp.concatenate([top, jnp.where(lane < GS, 0.0, pltpu.roll(top, GS, 1))], axis=0)


def diag_pair(first, second):
    zero = jnp.zeros((GS, GS), F32)
    return jnp.concatenate(
        [
            jnp.concatenate([first, zero], axis=1),
            jnp.concatenate([zero, second], axis=1),
        ],
        axis=0,
    )


def whiten_terms(packed, colors, total_pix):
    row = lax.broadcasted_iota(jnp.int32, (GS, GS), 0)
    col = lax.broadcasted_iota(jnp.int32, (GS, GS), 1)
    eye = jnp.where(row == col, 1.0, 0.0).astype(F32)
    cross = packed[:, COUT:].T
    tops, fulls, traces, crosses = [], [], [], []
    for group in range(2):
        sigma = packed[:, group * GS : (group + 1) * GS] * (1.0 / total_pix) + EPSILON * eye
        trace = jnp.sum(jnp.sum(sigma * eye, axis=1, keepdims=True), axis=0, keepdims=True)
        along = cross[group * GS : (group + 1) * GS]
        grad = exact(colors[group].T, along)
        tops.append(jnp.concatenate([sigma / trace, grad], axis=1))
        fulls.append(upper(tops[-1]))
        traces.append(trace)
        crosses.append(along)
    wide_eye = jnp.concatenate([eye, jnp.zeros((GS, GS), F32)], axis=1)
    states = [1.5 * wide_eye - 0.5 * top for top in tops]
    for _ in range(NS_ITERS - 1):
        squares = [exact(state, upper(state)) for state in states]
        by_normed = [exact(state, full) for state, full in zip(states, fulls)]
        cubes = [exact(square, upper(term)) for square, term in zip(squares, by_normed)]
        states = [1.5 * state - 0.5 * cube for state, cube in zip(states, cubes)]
    found = []
    for group in range(2):
        trace = traces[group]
        root = lax.rsqrt(trace)
        estimate, slope = states[group][:, :GS], states[group][:, GS:]
        normed, grad = tops[group][:, :GS], tops[group][:, GS:]
        scalar = slope * normed + 0.5 * grad * estimate
        scalar = jnp.sum(jnp.sum(scalar, axis=1, keepdims=True), axis=0, keepdims=True)
        sigma_grad = (slope - eye * scalar) * (root / trace)
        both = (sigma_grad + sigma_grad.T) * (1.0 / total_pix)
        whitener = estimate * root
        colored_by = exact(colors[group], whitener)
        color_sum = exact(crosses[group], whitener, ((1,), (1,)))
        found.append((colored_by, both, color_sum))
    return found


def block_kernel(
    total_pix,
    images,
    kernel,
    colors_in,
    offset_in,
    upstream,
    colored,
    grad_images,
    kernel_grad,
    color_grad,
    img,
    x3,
    wf,
    wb,
    colors,
    offset,
    imgt,
    pg3,
    pg_halo,
    base,
    sums,
    moments,
    rhi,
    rlo,
    consts,
    stat_src,
    stat_a,
    stat_p,
    stat_all,
    gk,
    rx_core,
    rx_plane,
    rx_line,
    full,
    load_sem,
    weight_sem,
    halo_send,
    halo_recv,
    oct_send,
    oct_recv,
    plane_send,
    plane_recv,
    back_send,
    back_recv,
    pg_send,
    pg_recv,
    gk_core_send,
    gk_core_recv,
    gk_line_send,
    gk_line_recv,
    gk_plane_send,
    gk_plane_recv,
):
    dp = lax.axis_index("dp")
    y = lax.axis_index("rows")
    x = dp // (RING * 2)
    z = (dp // 2) % RING
    core = dp % 2
    octet = x * 2 + core
    spot = y * RING + z
    inner = BAND - 2
    has_up = y > 0
    has_down = y < RING - 1

    def remote(src, dst, send, recv, device):
        return pltpu.make_async_remote_copy(
            src_ref=src,
            dst_ref=dst,
            send_sem=send,
            recv_sem=recv,
            device_id=device,
            device_id_type=MESH,
        )

    def oct_device(index):
        return (((index // 2) * RING + z) * 2 + index % 2, y)

    def plane_device(index):
        return ((x * RING + index % RING) * 2 + core, index // RING)

    up_device = (dp, (y + RING - 1) % RING)
    down_device = (dp, (y + 1) % RING)
    other_core = (dp + 1 - 2 * core, y)

    weight_loads = [
        pltpu.make_async_copy(
            kernel.at[a, c],
            wf.at[pl.ds(a * CIN, CIN), pl.ds(c * COUT, COUT)],
            weight_sem.at[a * 3 + c],
        )
        for a in range(3)
        for c in range(3)
    ] + [
        pltpu.make_async_copy(colors_in, colors, weight_sem.at[9]),
        pltpu.make_async_copy(offset_in, offset, weight_sem.at[10]),
    ]

    def load(b):
        return pltpu.make_async_copy(images.at[b], img.at[b, pl.ds(1, BAND)], load_sem.at[b])

    up_load = pltpu.make_async_copy(
        upstream, x3.at[:, :, :, pl.ds(2 * COUT, COUT)], load_sem.at[IMGS]
    )

    barrier = pltpu.get_barrier_semaphore()
    for k in range(1, PLANE):
        pl.semaphore_signal(
            barrier, inc=1, device_id=plane_device((spot + k) % PLANE), device_id_type=MESH
        )
    for k in range(1, OCT):
        pl.semaphore_signal(
            barrier, inc=1, device_id=oct_device((octet + k) % OCT), device_id_type=MESH
        )
    for copy in weight_loads:
        copy.start()
    for b in range(IMGS):
        load(b).start()
    up_load.start()

    @pl.when(y == 0)
    def _():
        img[:, 0] = jnp.zeros((IMGS, WID, CIN), BF16)
        pg3[:, 0] = jnp.zeros((IMGS, WID, ONE_ROW), BF16)

    @pl.when(y == RING - 1)
    def _():
        img[:, BAND + 1] = jnp.zeros((IMGS, WID, CIN), BF16)
        pg3[:, BAND + 1] = jnp.zeros((IMGS, WID, ONE_ROW), BF16)

    sums[...] = jnp.zeros_like(sums)
    moments[...] = jnp.zeros_like(moments)
    pl.semaphore_wait(barrier, OCT - 1 + PLANE - 1)

    def halo_up(b):
        return remote(
            images.at[b, 0],
            img.at[b, BAND + 1],
            halo_send.at[0, b],
            halo_recv.at[0, b],
            up_device,
        )

    def halo_down(b):
        return remote(
            images.at[b, BAND - 1],
            img.at[b, 0],
            halo_send.at[1, b],
            halo_recv.at[1, b],
            down_device,
        )

    for b in range(IMGS):

        @pl.when(has_up)
        def _():
            halo_up(b).start()

        @pl.when(has_down)
        def _():
            halo_down(b).start()

    for copy in weight_loads:
        copy.wait()
    up_load.wait()

    def conv(lhs):
        out = fast(lhs, wf[...])
        return (
            from_left(out[:, :COUT])
            + out[:, COUT : 2 * COUT]
            + from_right(out[:, 2 * COUT :])
        )

    def absorb(block, ups):
        apart = block - base[0:1, :]
        high = apart.astype(BF16)
        low = (apart - high.astype(F32)).astype(BF16)
        sums[:, :COUT] = sums[:, :COUT] + apart.reshape(-1, 8, COUT).sum(axis=0)
        sums[:, COUT:] = sums[:, COUT:] + ups.astype(F32).reshape(-1, 8, COUT).sum(axis=0)
        moments[...] = moments[...] + fast(high.T, jnp.concatenate([high, ups], axis=1))
        return jnp.concatenate([low, high], axis=1)

    def inner_conv(b):
        load(b).wait()
        return conv(
            jnp.concatenate(
                [img[b, pl.ds(1 + a, inner)].reshape(inner * WID, CIN) for a in range(3)],
                axis=1,
            )
        )

    def inner_absorb(b, block):
        ups = x3[b, pl.ds(1, inner), :, 2 * COUT :].reshape(inner * WID, COUT)
        both = absorb(block, ups)
        x3[b, pl.ds(1, inner), :, : 2 * COUT] = both.reshape(inner, WID, 2 * COUT)

    first = inner_conv(0)
    base[...] = jnp.broadcast_to(
        jnp.sum(first, axis=0, keepdims=True) * (1.0 / (inner * WID)), (8, COUT)
    )
    inner_absorb(0, first)

    @pl.loop(1, IMGS)
    def _(b):
        inner_absorb(b, inner_conv(b))

    for a in range(3):
        for c in range(3):
            tap = wf[a * CIN : (a + 1) * CIN, c * COUT : (c + 1) * COUT]
            wb[a * ONE_ROW + c * COUT : a * ONE_ROW + (c + 1) * COUT, :] = tap.T
    for b in range(IMGS):
        for h in range(BAND):
            start = (b * BAND + h) * WID
            imgt[:, start : start + WID] = img[b, h + 1].T

    @pl.loop(0, IMGS)
    def _(b):
        @pl.when(has_down)
        def _():
            halo_up(b).wait_recv()

        @pl.when(has_up)
        def _():
            halo_down(b).wait_recv()

        block = conv(
            jnp.concatenate(
                [
                    jnp.concatenate([img[b, a], img[b, BAND - 1 + a]], axis=0)
                    for a in range(3)
                ],
                axis=1,
            )
        )
        ups = jnp.concatenate(
            [x3[b, 0, :, 2 * COUT :], x3[b, BAND - 1, :, 2 * COUT :]], axis=0
        )
        both = absorb(block, ups)
        x3[b, 0, :, : 2 * COUT] = both[:WID]
        x3[b, BAND - 1, :, : 2 * COUT] = both[WID:]

    own = jnp.sum(sums[...], axis=0, keepdims=True) * (1.0 / PIX)
    drift = own[:, :COUT]
    column = jnp.broadcast_to(drift, (COUT, COUT)).T
    packed = pack(
        moments[...] - float(PIX) * jnp.concatenate([column, column], axis=1) * own
    )
    own_mean = jnp.concatenate([drift + base[0:1, :], own[:, COUT:]], axis=1)
    wide_own = jnp.broadcast_to(own_mean, (8, 2 * COUT))
    for slot in range(OCT):
        stat_src[slot, 0:8] = packed[slot * 8 : slot * 8 + 8]
        stat_src[slot, 8:16] = wide_own

    copies = []
    for k in range(1, OCT):
        target = (octet + k) % OCT
        copies.append(
            remote(
                stat_src.at[target],
                stat_a.at[octet],
                oct_send.at[k - 1],
                oct_recv.at[k - 1],
                oct_device(target),
            )
        )
    for copy in copies:
        copy.start()
    stat_a[octet] = stat_src[octet]
    for copy in copies:
        copy.wait()
    rows = stat_a[0, 0:8]
    means = stat_a[0, 8:16]
    index = lax.broadcasted_iota(jnp.int32, means.shape, 0)
    for slot in range(1, OCT):
        rows = rows + stat_a[slot, 0:8]
        means = jnp.where(index == slot, stat_a[slot, 8:16], means)
    stat_p[spot, 0:8] = rows
    stat_p[spot, 8:16] = means
    copies = [
        remote(
            stat_p.at[spot],
            stat_p.at[spot],
            plane_send.at[k - 1],
            plane_recv.at[k - 1],
            plane_device((spot + k) % PLANE),
        )
        for k in range(1, PLANE)
    ]
    for copy in copies:
        copy.start()
    for copy in copies:
        copy.wait()
    rows = stat_p[0, 0:8]
    for slot in range(1, PLANE):
        rows = rows + stat_p[slot, 0:8]
    stat_all[octet] = rows
    copies = [
        remote(
            stat_all.at[octet],
            stat_all.at[octet],
            back_send.at[k - 1],
            back_recv.at[k - 1],
            oct_device((octet + k) % OCT),
        )
        for k in range(1, OCT)
    ]
    for copy in copies:
        copy.start()
    means = jnp.concatenate([stat_p[slot, 8:16] for slot in range(PLANE)], axis=0)
    count = OCT * PLANE
    all_mean = jnp.broadcast_to(
        jnp.sum(means, axis=0, keepdims=True) * (1.0 / count), (8, 2 * COUT)
    )
    apart = means - all_mean[0:1, :]
    between = pack(exact(apart[:, :COUT].T, apart)) * float(PIX)
    for copy in copies:
        copy.wait()
    packed = (
        jnp.concatenate([stat_all[slot] for slot in range(OCT)], axis=0) + between
    )

    (t0, b0, s0), (t1, b1, s1) = whiten_terms(packed, colors, total_pix)
    by_x = jnp.concatenate([diag_pair(t0.T, t1.T), diag_pair(b0, b1)], axis=1)
    by_up = jnp.concatenate([jnp.zeros((COUT, COUT), F32), diag_pair(t0, t1)], axis=1)
    x_high, up_high = by_x.astype(BF16), by_up.astype(BF16)
    rhi[0:COUT] = x_high
    rhi[COUT : 2 * COUT] = x_high
    rhi[2 * COUT :] = up_high
    rlo[0:COUT] = (by_x - x_high.astype(F32)).astype(BF16)
    rlo[COUT:] = (by_up - up_high.astype(F32)).astype(BF16)
    shift = base[...] - all_mean[:, :COUT]
    level = exact(shift, by_x) - exact(all_mean[:, COUT:], by_up)
    consts[:, :COUT] = level[:, :COUT] + offset[...]
    consts[:, COUT:] = level[:, COUT:]

    def spread(block):
        return jnp.concatenate(
            [from_right(block).astype(BF16), block.astype(BF16), from_left(block).astype(BF16)],
            axis=1,
        )

    def finish(lhs):
        out = fast(lhs, rhi[...]) + fast(lhs[:, COUT:], rlo[...]) + consts[0:1, :]
        return out[:, :COUT].astype(BF16), spread(out[:, COUT:])

    def pg_up(b):
        return remote(
            pg3.at[b, 1, :, pl.ds(COUT, COUT)],
            pg_halo.at[1, b],
            pg_send.at[0, b],
            pg_recv.at[0, b],
            up_device,
        )

    def pg_down(b):
        return remote(
            pg3.at[b, BAND, :, pl.ds(COUT, COUT)],
            pg_halo.at[0, b],
            pg_send.at[1, b],
            pg_recv.at[1, b],
            down_device,
        )

    @pl.loop(0, IMGS)
    def _(b):
        shown, grads = finish(jnp.concatenate([x3[b, 0], x3[b, BAND - 1]], axis=0))
        colored[b, 0] = shown[:WID]
        colored[b, BAND - 1] = shown[WID:]
        pg3[b, 1] = grads[:WID]
        pg3[b, BAND] = grads[WID:]

        @pl.when(has_up)
        def _():
            pg_up(b).start()

        @pl.when(has_down)
        def _():
            pg_down(b).start()

    @pl.loop(0, IMGS)
    def _(b):
        shown, grads = finish(x3[b, pl.ds(1, inner)].reshape(inner * WID, 3 * COUT))
        colored[b, pl.ds(1, inner)] = shown.reshape(inner, WID, COUT)
        pg3[b, pl.ds(2, inner)] = grads.reshape(inner, WID, ONE_ROW)

    color_grad[0] = s0 * (1.0 / math.sqrt(total_pix))
    color_grad[1] = s1 * (1.0 / math.sqrt(total_pix))

    def rows_product(image_row, grad_row, rows):
        lhs = jnp.concatenate(
            [
                imgt[:, (b * BAND + image_row) * WID : (b * BAND + image_row + rows) * WID]
                for b in range(IMGS)
            ],
            axis=1,
        )
        rhs = jnp.concatenate(
            [
                pg3[b, grad_row : grad_row + rows].reshape(rows * WID, ONE_ROW)
                for b in range(IMGS)
            ],
            axis=0,
        )
        return fast(lhs, rhs)

    half = CIN // 2
    piece = half // PLANE

    def rows_at(start, size):
        return pl.ds(pl.multiple_of(start, size), size)

    mine = rows_at(core * half, half)
    theirs = rows_at((1 - core) * half, half)
    my_piece = rows_at(core * half + spot * piece, piece)
    flying = {}

    def start(part, copies):
        for copy in copies:
            copy.start()
        flying[part] = copies

    def settle(part):
        for copy in flying[part]:
            copy.wait()

    def plane_copies(part, stage, src, dst):
        return [
            remote(
                src((spot + k) % PLANE),
                dst(k),
                gk_plane_send.at[part, stage, k - 1],
                gk_plane_recv.at[part, stage, k - 1],
                plane_device((spot + k) % PLANE),
            )
            for k in range(1, PLANE)
        ]

    def step(part, stage):
        if stage > 0:
            settle(part)
        if stage == 0:
            start(
                part,
                [
                    remote(
                        gk.at[part, theirs],
                        rx_core.at[part],
                        gk_core_send.at[part, 0],
                        gk_core_recv.at[part, 0],
                        other_core,
                    )
                ],
            )
        elif stage == 1:
            gk[part, mine] = gk[part, mine] + rx_core[part]
            start(
                part,
                plane_copies(
                    part,
                    0,
                    lambda spot: gk.at[part, rows_at(core * half + spot * piece, piece)],
                    lambda k: rx_plane.at[part, k - 1],
                ),
            )
        elif stage == 2:
            held = gk[part, my_piece]
            for k in range(PLANE - 1):
                held = held + rx_plane[part, k]
            rx_line[part, x] = held
            start(
                part,
                [
                    remote(
                        rx_line.at[part, x],
                        rx_line.at[part, x],
                        gk_line_send.at[part, k - 1],
                        gk_line_recv.at[part, k - 1],
                        oct_device(((x + k) % RING) * 2 + core),
                    )
                    for k in range(1, RING)
                ],
            )
        elif stage == 3:
            full[part, my_piece] = (rx_line[part, 0] + rx_line[part, 1]) + (
                rx_line[part, 2] + rx_line[part, 3]
            )
            start(
                part,
                plane_copies(
                    part,
                    1,
                    lambda spot: full.at[part, my_piece],
                    lambda k: full.at[part, my_piece],
                ),
            )
        elif stage == 4:
            start(
                part,
                [
                    remote(
                        full.at[part, mine],
                        full.at[part, mine],
                        gk_core_send.at[part, 1],
                        gk_core_recv.at[part, 1],
                        other_core,
                    )
                ],
            )
        elif stage == 5:
            for c in range(3):
                kernel_grad[part, c] = full[part, :, c * COUT : (c + 1) * COUT] * (
                    1.0 / math.sqrt(total_pix)
                )

    def image_grad(b):
        lhs = jnp.concatenate(
            [pg3[b, pl.ds(2 - a, BAND)].reshape(BAND * WID, ONE_ROW) for a in range(3)],
            axis=1,
        )
        grad_images[b] = fast(lhs, wb[...]).astype(BF16).reshape(BAND, WID, CIN)

    gk[1] = rows_product(0, 1, BAND)
    step(1, 0)
    gk[0] = rows_product(0, 2, BAND - 1)

    @pl.loop(0, IMGS)
    def _(b):
        @pl.when(has_down)
        def _():
            pg_up(b).wait_recv()
            pg3[b, BAND + 1] = spread(pg_halo[1, b].astype(F32))

    gk[0] = gk[0] + rows_product(BAND - 1, BAND + 1, 1)
    step(0, 0)
    step(1, 1)
    gk[2] = rows_product(1, 1, BAND - 1)

    @pl.loop(0, IMGS)
    def _(b):
        @pl.when(has_up)
        def _():
            pg_down(b).wait_recv()
            pg3[b, 0] = spread(pg_halo[0, b].astype(F32))

    gk[2] = gk[2] + rows_product(0, 0, 1)
    step(2, 0)
    step(0, 1)
    image_grad(0)
    step(2, 1)
    image_grad(1)
    step(1, 2)
    image_grad(2)
    image_grad(3)
    step(0, 2)
    image_grad(4)
    step(1, 3)
    image_grad(5)
    step(2, 2)
    step(0, 3)
    step(2, 3)
    step(1, 4)
    step(0, 4)
    step(1, 5)
    step(2, 4)
    step(0, 5)
    step(2, 5)

    @pl.loop(0, IMGS)
    def _(b):
        @pl.when(has_up)
        def _():
            halo_up(b).wait_send()
            pg_up(b).wait_send()

        @pl.when(has_down)
        def _():
            halo_down(b).wait_send()
            pg_down(b).wait_send()


def place_kernel(*refs):
    count = (len(refs) - 1) // 2
    copies = [
        pltpu.make_async_copy(refs[i], refs[count + i], refs[-1].at[i]) for i in range(count)
    ]
    for copy in copies:
        copy.start()
    for copy in copies:
        copy.wait()


def body(images, kernel, colors, offset, upstream):
    total_pix = PIX * lax.axis_size("dp") * lax.axis_size("rows")
    anywhere = pl.BlockSpec(memory_space=pl.ANY)
    outside = pl.BlockSpec(memory_space=pltpu.HBM)
    local = pl.BlockSpec(memory_space=pltpu.VMEM)
    dma = pltpu.SemaphoreType.DMA
    shapes = (
        jax.ShapeDtypeStruct((IMGS, BAND, WID, COUT), BF16),
        jax.ShapeDtypeStruct((IMGS, BAND, WID, CIN), BF16),
        jax.ShapeDtypeStruct((3, 3, CIN, COUT), F32),
        jax.ShapeDtypeStruct((2, GS, GS), F32),
    )
    results = pl.pallas_call(
        functools.partial(block_kernel, total_pix),
        out_shape=shapes,
        in_specs=[outside] * 5,
        out_specs=(local, local, local, local),
        scratch_shapes=[
            pltpu.VMEM((IMGS, BAND + 2, WID, CIN), BF16),
            pltpu.VMEM((IMGS, BAND, WID, 3 * COUT), BF16),
            pltpu.VMEM((3 * CIN, ONE_ROW), BF16),
            pltpu.VMEM((3 * ONE_ROW, CIN), BF16),
            pltpu.VMEM((2, GS, GS), F32),
            pltpu.VMEM((1, COUT), F32),
            pltpu.VMEM((CIN, PIX), BF16),
            pltpu.VMEM((IMGS, BAND + 2, WID, ONE_ROW), BF16),
            pltpu.VMEM((2, IMGS, WID, COUT), BF16),
            pltpu.VMEM((8, COUT), F32),
            pltpu.VMEM((8, 2 * COUT), F32),
            pltpu.VMEM((COUT, 2 * COUT), F32),
            pltpu.VMEM((3 * COUT, 2 * COUT), BF16),
            pltpu.VMEM((2 * COUT, 2 * COUT), BF16),
            pltpu.VMEM((8, 2 * COUT), F32),
            pltpu.VMEM((OCT, 16, 2 * COUT), F32),
            pltpu.VMEM((OCT, 16, 2 * COUT), F32),
            pltpu.VMEM((PLANE, 16, 2 * COUT), F32),
            pltpu.VMEM((OCT, 8, 2 * COUT), F32),
            pltpu.VMEM((3, CIN, ONE_ROW), F32),
            pltpu.VMEM((3, CIN // 2, ONE_ROW), F32),
            pltpu.VMEM((3, PLANE - 1, CIN // 32, ONE_ROW), F32),
            pltpu.VMEM((3, RING, CIN // 32, ONE_ROW), F32),
            pltpu.VMEM((3, CIN, ONE_ROW), F32),
            dma((IMGS + 1,)),
            dma((11,)),
            dma((2, IMGS)),
            dma((2, IMGS)),
            dma((OCT - 1,)),
            dma((OCT - 1,)),
            dma((PLANE - 1,)),
            dma((PLANE - 1,)),
            dma((OCT - 1,)),
            dma((OCT - 1,)),
            dma((2, IMGS)),
            dma((2, IMGS)),
            dma((3, 2)),
            dma((3, 2)),
            dma((3, RING - 1)),
            dma((3, RING - 1)),
            dma((3, 2, PLANE - 1)),
            dma((3, 2, PLANE - 1)),
        ],
        compiler_params=pltpu.CompilerParams(
            collective_id=0, has_side_effects=True, vmem_limit_bytes=40 * 1024 * 1024
        ),
    )(
        *[
            pltpu.with_memory_space_constraint(given, pltpu.HBM)
            for given in (images, kernel, colors, offset.reshape(1, COUT), upstream)
        ]
    )
    return pl.pallas_call(
        place_kernel,
        out_shape=shapes,
        in_specs=[anywhere] * 4,
        out_specs=(anywhere,) * 4,
        scratch_shapes=[dma((4,))],
        compiler_params=pltpu.CompilerParams(vmem_limit_bytes=1024 * 1024),
    )(*results)


def solution(mesh):
    placed = (P("dp", "rows", None, None), P(), P(), P(), P("dp", "rows", None, None))
    return jax.shard_map(
        body,
        mesh=mesh,
        in_specs=placed,
        out_specs=(P("dp", "rows", None, None), P("dp", "rows", None, None), P(), P()),
        check_vma=False,
    )
```

time: 92.2 us -> 75.4 us (0.82)
  Pallas kernels: 83.3 us -> 74.5 us
  local copies, waits for them, and re-layouts: 6.93 us -> 0 us
  other arithmetic: 1.17 us -> 0 us
    pallas_call x1 -> x2, Pallas kernels: 83.3 us -> 74.5 us  [the longest x1 71.9 us: body(): pl.pallas_call(functools.partial(block_kernel, total_pix), out_shape=shap...]
    unnamed x8 -> x0, local copies, waits for them, and re-layouts: 6.56 us -> none
    mul x1 -> x0, other arithmetic: 1.17 us -> none  [body(): kernel_sum.reshape(3, CIN, 3, COUT).transpose(0, 2, 1, 3).astype(F32)]
where the time goes in v2:
time: 75.4 us; the launch traced here: 75.3 us
  Pallas kernels  74.5 us (99%)
  between operations  0.8 us (1%)
    pallas_call x1, Pallas kernels, body(): pl.pallas_call(functools.partial(block_kernel, total_pix), out_shape=shap...  71.9 us
    pallas_call x1, Pallas kernels, body(): pl.pallas_call(place_kernel, out_shape=shapes, in_specs=[anywhere] * 4, o...  2.61 us

profile of v2, /device:TPU:1, one launch (start us, length us, event | category | flops | bytes accessed | tf_op | source)
XLA Modules:
  0.0 75.3 jit_solution(8469286150265554444)
XLA Ops:
  0.6 71.9 %shard_map.84 = (bf16[6,8,128,128]{3,2,1,0:T(8,128)(2,1)S(1)}, bf16[6,8,128,256]{3,2,1,0:T(8,128)(2,1)S(1)}, f32[3,3,256,128]{3,2,1,0:T(8,128)S(1)}, f32[2,64,64]{2,1,0:T(8,128)S(1)}) custom-call(bf16[6,8,128,256]{3,2,1,0:T(8,128)(2,1)} %images.1, bf16[3,3,256,128]{3,2,1,0:T(8,128)(2,1)} %kernel.1, f32[2,64,64]{2,1,0:T(8,128)} %colors_in.1, ...), custom_call_target="tpu_custom_call" | custom-call | tf_op jit(solution)/shard_map/pallas_call | solution.py:710
  72.5 2.6 %shard_map.85 = (bf16[6,8,128,128]{3,2,1,0:T(8,128)(2,1)}, bf16[6,8,128,256]{3,2,1,0:T(8,128)(2,1)}, f32[3,3,256,128]{3,2,1,0:T(8,128)}, f32[2,64,64]{2,1,0:T(8,128)}) custom-call(bf16[6,8,128,128]{3,2,1,0:T(8,128)(2,1)S(1)} %get-tuple-element.8.refs_0_, bf16[6,8,128,256]{3,2,1,0:T(8,128)(2,1)S(1)} %get-tuple-element.9.refs_1_, ...), custom_call_target="tpu_custom_call" | custom-call | tf_op jit(solution)/shard_map/pallas_call | solution.py:768

commit v3 on v2

--- a/solution.py
+++ b/solution.py
@@ -64,7 +64,7 @@
     )
 
 
-def whiten_terms(packed, colors, total_pix):
+def whiten_terms(packed, colors, total_pix, between):
     row = lax.broadcasted_iota(jnp.int32, (GS, GS), 0)
     col = lax.broadcasted_iota(jnp.int32, (GS, GS), 1)
     eye = jnp.where(row == col, 1.0, 0.0).astype(F32)
@@ -81,7 +81,9 @@
         crosses.append(along)
     wide_eye = jnp.concatenate([eye, jnp.zeros((GS, GS), F32)], axis=1)
     states = [1.5 * wide_eye - 0.5 * top for top in tops]
-    for _ in range(NS_ITERS - 1):
+    for repeat in range(NS_ITERS - 1):
+        if repeat == 2:
+            between()
         squares = [exact(state, upper(state)) for state in states]
         by_normed = [exact(state, full) for state, full in zip(states, fulls)]
         cubes = [exact(square, upper(term)) for square, term in zip(squares, by_normed)]
@@ -121,6 +123,8 @@
     colors,
     offset,
     imgt,
+    window,
+    window_col,
     pg3,
     pg_halo,
     base,
@@ -128,15 +132,19 @@
     moments,
     rhi,
     rlo,
+    mix,
     consts,
     stat_src,
     stat_a,
     stat_p,
     stat_all,
+    spare,
     gk,
     rx_core,
-    rx_plane,
-    rx_line,
+    rx_first,
+    held,
+    rx_second,
+    rx_third,
     full,
     load_sem,
     weight_sem,
@@ -154,8 +162,6 @@
     gk_core_recv,
     gk_line_send,
     gk_line_recv,
-    gk_plane_send,
-    gk_plane_recv,
 ):
     dp = lax.axis_index("dp")
     y = lax.axis_index("rows")
@@ -314,10 +320,18 @@
         for c in range(3):
             tap = wf[a * CIN : (a + 1) * CIN, c * COUT : (c + 1) * COUT]
             wb[a * ONE_ROW + c * COUT : a * ONE_ROW + (c + 1) * COUT, :] = tap.T
-    for b in range(IMGS):
-        for h in range(BAND):
-            start = (b * BAND + h) * WID
-            imgt[:, start : start + WID] = img[b, h + 1].T
+    window[...] = jnp.zeros_like(window)
+
+    def turn(b, row):
+        values = img[b, row].astype(F32)
+        for c, moved in enumerate((from_left(values), values, from_right(values))):
+            imgt[b, row, c * CIN : (c + 1) * CIN, :] = moved.astype(BF16).T
+            window[row, c] = window[row, c] + moved.reshape(-1, 8, CIN).sum(axis=0)
+
+    @pl.loop(0, IMGS)
+    def _(b):
+        for row in range(1, BAND + 1):
+            turn(b, row)
 
     @pl.loop(0, IMGS)
     def _(b):
@@ -344,180 +358,25 @@
         both = absorb(block, ups)
         x3[b, 0, :, : 2 * COUT] = both[:WID]
         x3[b, BAND - 1, :, : 2 * COUT] = both[WID:]
-
-    own = jnp.sum(sums[...], axis=0, keepdims=True) * (1.0 / PIX)
-    drift = own[:, :COUT]
-    column = jnp.broadcast_to(drift, (COUT, COUT)).T
-    packed = pack(
-        moments[...] - float(PIX) * jnp.concatenate([column, column], axis=1) * own
-    )
-    own_mean = jnp.concatenate([drift + base[0:1, :], own[:, COUT:]], axis=1)
-    wide_own = jnp.broadcast_to(own_mean, (8, 2 * COUT))
-    for slot in range(OCT):
-        stat_src[slot, 0:8] = packed[slot * 8 : slot * 8 + 8]
-        stat_src[slot, 8:16] = wide_own
-
-    copies = []
-    for k in range(1, OCT):
-        target = (octet + k) % OCT
-        copies.append(
-            remote(
-                stat_src.at[target],
-                stat_a.at[octet],
-                oct_send.at[k - 1],
-                oct_recv.at[k - 1],
-                oct_device(target),
-            )
-        )
-    for copy in copies:
-        copy.start()
-    stat_a[octet] = stat_src[octet]
-    for copy in copies:
-        copy.wait()
-    rows = stat_a[0, 0:8]
-    means = stat_a[0, 8:16]
-    index = lax.broadcasted_iota(jnp.int32, means.shape, 0)
-    for slot in range(1, OCT):
-        rows = rows + stat_a[slot, 0:8]
-        means = jnp.where(index == slot, stat_a[slot, 8:16], means)
-    stat_p[spot, 0:8] = rows
-    stat_p[spot, 8:16] = means
-    copies = [
-        remote(
-            stat_p.at[spot],
-            stat_p.at[spot],
-            plane_send.at[k - 1],
-            plane_recv.at[k - 1],
-            plane_device((spot + k) % PLANE),
-        )
-        for k in range(1, PLANE)
-    ]
-    for copy in copies:
-        copy.start()
-    for copy in copies:
-        copy.wait()
-    rows = stat_p[0, 0:8]
-    for slot in range(1, PLANE):
-        rows = rows + stat_p[slot, 0:8]
-    stat_all[octet] = rows
-    copies = [
-        remote(
-            stat_all.at[octet],
-            stat_all.at[octet],
-            back_send.at[k - 1],
-            back_recv.at[k - 1],
-            oct_device((octet + k) % OCT),
-        )
-        for k in range(1, OCT)
-    ]
-    for copy in copies:
-        copy.start()
-    means = jnp.concatenate([stat_p[slot, 8:16] for slot in range(PLANE)], axis=0)
-    count = OCT * PLANE
-    all_mean = jnp.broadcast_to(
-        jnp.sum(means, axis=0, keepdims=True) * (1.0 / count), (8, 2 * COUT)
-    )
-    apart = means - all_mean[0:1, :]
-    between = pack(exact(apart[:, :COUT].T, apart)) * float(PIX)
-    for copy in copies:
-        copy.wait()
-    packed = (
-        jnp.concatenate([stat_all[slot] for slot in range(OCT)], axis=0) + between
-    )
-
-    (t0, b0, s0), (t1, b1, s1) = whiten_terms(packed, colors, total_pix)
-    by_x = jnp.concatenate([diag_pair(t0.T, t1.T), diag_pair(b0, b1)], axis=1)
-    by_up = jnp.concatenate([jnp.zeros((COUT, COUT), F32), diag_pair(t0, t1)], axis=1)
-    x_high, up_high = by_x.astype(BF16), by_up.astype(BF16)
-    rhi[0:COUT] = x_high
-    rhi[COUT : 2 * COUT] = x_high
-    rhi[2 * COUT :] = up_high
-    rlo[0:COUT] = (by_x - x_high.astype(F32)).astype(BF16)
-    rlo[COUT:] = (by_up - up_high.astype(F32)).astype(BF16)
-    shift = base[...] - all_mean[:, :COUT]
-    level = exact(shift, by_x) - exact(all_mean[:, COUT:], by_up)
-    consts[:, :COUT] = level[:, :COUT] + offset[...]
-    consts[:, COUT:] = level[:, COUT:]
-
-    def spread(block):
-        return jnp.concatenate(
-            [from_right(block).astype(BF16), block.astype(BF16), from_left(block).astype(BF16)],
-            axis=1,
-        )
-
-    def finish(lhs):
-        out = fast(lhs, rhi[...]) + fast(lhs[:, COUT:], rlo[...]) + consts[0:1, :]
-        return out[:, :COUT].astype(BF16), spread(out[:, COUT:])
-
-    def pg_up(b):
-        return remote(
-            pg3.at[b, 1, :, pl.ds(COUT, COUT)],
-            pg_halo.at[1, b],
-            pg_send.at[0, b],
-            pg_recv.at[0, b],
-            up_device,
-        )
-
-    def pg_down(b):
-        return remote(
-            pg3.at[b, BAND, :, pl.ds(COUT, COUT)],
-            pg_halo.at[0, b],
-            pg_send.at[1, b],
-            pg_recv.at[1, b],
-            down_device,
-        )
-
-    @pl.loop(0, IMGS)
-    def _(b):
-        shown, grads = finish(jnp.concatenate([x3[b, 0], x3[b, BAND - 1]], axis=0))
-        colored[b, 0] = shown[:WID]
-        colored[b, BAND - 1] = shown[WID:]
-        pg3[b, 1] = grads[:WID]
-        pg3[b, BAND] = grads[WID:]
-
-        @pl.when(has_up)
-        def _():
-            pg_up(b).start()
-
-        @pl.when(has_down)
-        def _():
-            pg_down(b).start()
-
-    @pl.loop(0, IMGS)
-    def _(b):
-        shown, grads = finish(x3[b, pl.ds(1, inner)].reshape(inner * WID, 3 * COUT))
-        colored[b, pl.ds(1, inner)] = shown.reshape(inner, WID, COUT)
-        pg3[b, pl.ds(2, inner)] = grads.reshape(inner, WID, ONE_ROW)
-
-    color_grad[0] = s0 * (1.0 / math.sqrt(total_pix))
-    color_grad[1] = s1 * (1.0 / math.sqrt(total_pix))
-
-    def rows_product(image_row, grad_row, rows):
-        lhs = jnp.concatenate(
-            [
-                imgt[:, (b * BAND + image_row) * WID : (b * BAND + image_row + rows) * WID]
-                for b in range(IMGS)
-            ],
-            axis=1,
-        )
-        rhs = jnp.concatenate(
-            [
-                pg3[b, grad_row : grad_row + rows].reshape(rows * WID, ONE_ROW)
-                for b in range(IMGS)
-            ],
-            axis=0,
-        )
-        return fast(lhs, rhs)
-
-    half = CIN // 2
-    piece = half // PLANE
+        turn(b, 0)
+        turn(b, BAND + 1)
+
+    orders = (("x", "y", "z"), ("y", "z", "x"), ("z", "x", "y"))
+    where = {"x": x, "y": y, "z": z}
+    half = 3 * CIN // 2
+    quarter = half // RING
+    piece = quarter // RING
 
     def rows_at(start, size):
-        return pl.ds(pl.multiple_of(start, size), size)
+        return pl.ds(pl.multiple_of(start, 8), size)
+
+    def axis_device(axis, index):
+        if axis == "x":
+            return oct_device(index * 2 + core)
+        return plane_device(index * RING + z if axis == "y" else y * RING + index)
 
     mine = rows_at(core * half, half)
     theirs = rows_at((1 - core) * half, half)
-    my_piece = rows_at(core * half + spot * piece, piece)
     flying = {}
 
     def start(part, copies):
@@ -529,19 +388,24 @@
         for copy in flying[part]:
             copy.wait()
 
-    def plane_copies(part, stage, src, dst):
+    def line_copies(part, stage, src, dst):
+        axis = orders[part][(0, 1, 2, 1, 0)[stage]]
+        me = where[axis]
         return [
             remote(
-                src((spot + k) % PLANE),
+                src((me + k) % RING),
                 dst(k),
-                gk_plane_send.at[part, stage, k - 1],
-                gk_plane_recv.at[part, stage, k - 1],
-                plane_device((spot + k) % PLANE),
-            )
-            for k in range(1, PLANE)
+                gk_line_send.at[part, stage, k - 1],
+                gk_line_recv.at[part, stage, k - 1],
+                axis_device(axis, (me + k) % RING),
+            )
+            for k in range(1, RING)
         ]
 
     def step(part, stage):
+        first, second, third = (where[axis] for axis in orders[part])
+        my_quarter = rows_at(core * half + first * quarter, quarter)
+        my_piece = rows_at(core * half + first * quarter + second * piece, piece)
         if stage > 0:
             settle(part)
         if stage == 0:
@@ -561,45 +425,69 @@
             gk[part, mine] = gk[part, mine] + rx_core[part]
             start(
                 part,
-                plane_copies(
+                line_copies(
                     part,
                     0,
-                    lambda spot: gk.at[part, rows_at(core * half + spot * piece, piece)],
-                    lambda k: rx_plane.at[part, k - 1],
+                    lambda index: gk.at[part, rows_at(core * half + index * quarter, quarter)],
+                    lambda k: rx_first.at[part, k - 1],
                 ),
             )
         elif stage == 2:
-            held = gk[part, my_piece]
-            for k in range(PLANE - 1):
-                held = held + rx_plane[part, k]
-            rx_line[part, x] = held
+            held[part] = (
+                (gk[part, my_quarter] + rx_first[part, 0])
+                + (rx_first[part, 1] + rx_first[part, 2])
+            )
             start(
                 part,
-                [
-                    remote(
-                        rx_line.at[part, x],
-                        rx_line.at[part, x],
-                        gk_line_send.at[part, k - 1],
-                        gk_line_recv.at[part, k - 1],
-                        oct_device(((x + k) % RING) * 2 + core),
-                    )
-                    for k in range(1, RING)
-                ],
+                line_copies(
+                    part,
+                    1,
+                    lambda index: held.at[part, rows_at(index * piece, piece)],
+                    lambda k: rx_second.at[part, k - 1],
+                ),
             )
         elif stage == 3:
-            full[part, my_piece] = (rx_line[part, 0] + rx_line[part, 1]) + (
-                rx_line[part, 2] + rx_line[part, 3]
+            rx_third[part, third] = (
+                (held[part, rows_at(second * piece, piece)] + rx_second[part, 0])
+                + (rx_second[part, 1] + rx_second[part, 2])
             )
             start(
                 part,
-                plane_copies(
+                line_copies(
                     part,
-                    1,
-                    lambda spot: full.at[part, my_piece],
+                    2,
+                    lambda index: rx_third.at[part, third],
+                    lambda k: rx_third.at[part, third],
+                ),
+            )
+        elif stage == 4:
+            total = (rx_third[part, 0] + rx_third[part, 1]) + (
+                rx_third[part, 2] + rx_third[part, 3]
+            )
+            full[part, my_piece] = (
+                exact(total, mix[0 : 2 * COUT])
+                + window_col[part, my_piece] * mix[2 * COUT : 2 * COUT + 1]
+            )
+            start(
+                part,
+                line_copies(
+                    part,
+                    3,
+                    lambda index: full.at[part, my_piece],
                     lambda k: full.at[part, my_piece],
                 ),
             )
-        elif stage == 4:
+        elif stage == 5:
+            start(
+                part,
+                line_copies(
+                    part,
+                    4,
+                    lambda index: full.at[part, my_quarter],
+                    lambda k: full.at[part, my_quarter],
+                ),
+            )
+        elif stage == 6:
             start(
                 part,
                 [
@@ -612,11 +500,221 @@
                     )
                 ],
             )
-        elif stage == 5:
+        elif stage == 7:
             for c in range(3):
-                kernel_grad[part, c] = full[part, :, c * COUT : (c + 1) * COUT] * (
+                kernel_grad[part, c] = full[part, c * CIN : (c + 1) * CIN] * (
                     1.0 / math.sqrt(total_pix)
                 )
+
+    own = jnp.sum(sums[...], axis=0, keepdims=True) * (1.0 / PIX)
+    drift = own[:, :COUT]
+    column = jnp.broadcast_to(drift, (COUT, COUT)).T
+    packed = pack(
+        moments[...] - float(PIX) * jnp.concatenate([column, column], axis=1) * own
+    )
+    own_mean = jnp.concatenate([drift + base[0:1, :], own[:, COUT:]], axis=1)
+    index = lax.broadcasted_iota(jnp.int32, (8, 2 * COUT), 0)
+    taps = []
+    for a in range(3):
+        for c in range(3):
+            total = window[a, c]
+            for row in range(a + 1, a + BAND):
+                total = total + window[row, c]
+            taps.append(jnp.sum(total, axis=0, keepdims=True))
+    taps = taps + [jnp.zeros_like(taps[0])] * (2 * OCT - len(taps))
+    for slot in range(OCT):
+        stat_src[slot, 0:8] = packed[slot * 8 : slot * 8 + 8]
+        tail = jnp.where(index == 0, own_mean, 0.0)
+        tail = jnp.where(index == 1, taps[2 * slot], tail)
+        stat_src[slot, 8:16] = jnp.where(index == 2, taps[2 * slot + 1], tail)
+
+    def columns_of(rows):
+        place = lax.broadcasted_iota(jnp.int32, (2 * OCT, CIN), 0)
+        stacked = jnp.zeros((2 * OCT, CIN), F32)
+        for tap in range(9):
+            stacked = jnp.where(place == tap, rows[tap], stacked)
+        return stacked.T
+
+    round_one = []
+    for k in range(1, OCT):
+        target = (octet + k) % OCT
+        round_one.append(
+            remote(
+                stat_src.at[target],
+                stat_a.at[octet],
+                oct_send.at[k - 1],
+                oct_recv.at[k - 1],
+                oct_device(target),
+            )
+        )
+    for copy in round_one:
+        copy.start()
+    stat_a[octet] = stat_src[octet]
+
+    own_cols = columns_of(taps)
+
+    def weight_part(a):
+        lhs = jnp.concatenate([imgt[b, a + h] for b in range(IMGS) for h in range(BAND)], axis=1)
+        gk[a] = fast(lhs, x3[:, :, :, COUT:].reshape(PIX, 2 * COUT))
+        for c in range(3):
+            column = own_cols[:, a * 3 + c : a * 3 + c + 1]
+            rows = slice(c * CIN, (c + 1) * CIN)
+            gk[a, rows, :COUT] = gk[a, rows, :COUT] + column * base[0:1, :]
+
+    weight_part(1)
+    step(1, 0)
+    weight_part(0)
+    step(0, 0)
+    for copy in round_one:
+        copy.wait()
+
+    def spread_of(means, pixels):
+        middle = jnp.sum(means, axis=0, keepdims=True) * (1.0 / means.shape[0])
+        apart = means - middle
+        return middle, pack(exact(apart[:, :COUT].T, apart)) * float(pixels)
+
+    def tails_of(buf, count):
+        place = lax.broadcasted_iota(jnp.int32, (count, 2 * COUT), 0)
+        rows, tail = buf[0, 0:8], buf[0, 8:16]
+        means = jnp.broadcast_to(buf[0, 8:9], (count, 2 * COUT))
+        for slot in range(1, count):
+            rows = rows + buf[slot, 0:8]
+            tail = tail + buf[slot, 8:16]
+            means = jnp.where(place == slot, buf[slot, 8:9], means)
+        return rows, tail, means
+
+    rows, tail, means = tails_of(stat_a, OCT)
+    middle, between = spread_of(means, PIX)
+    for slot in range(OCT):
+        spare[slot] = between[slot * 8 : slot * 8 + 8]
+    stat_p[spot, 0:8] = rows + spare[octet]
+    stat_p[spot, 8:16] = jnp.where(index == 0, middle, tail)
+    round_two = [
+        remote(
+            stat_p.at[spot],
+            stat_p.at[spot],
+            plane_send.at[k - 1],
+            plane_recv.at[k - 1],
+            plane_device((spot + k) % PLANE),
+        )
+        for k in range(1, PLANE)
+    ]
+    for copy in round_two:
+        copy.start()
+    step(1, 1)
+    weight_part(2)
+    step(2, 0)
+    step(0, 1)
+    step(2, 1)
+    for copy in round_two:
+        copy.wait()
+    rows, tail, means = tails_of(stat_p, PLANE)
+    stat_all[octet, 0:8] = rows
+    stat_all[octet, 8:16] = tail
+    round_three = [
+        remote(
+            stat_all.at[octet],
+            stat_all.at[octet],
+            back_send.at[k - 1],
+            back_recv.at[k - 1],
+            oct_device((octet + k) % OCT),
+        )
+        for k in range(1, OCT)
+    ]
+    for copy in round_three:
+        copy.start()
+    step(1, 2)
+    middle, between = spread_of(means, PIX * OCT)
+    all_mean = jnp.broadcast_to(middle, (8, 2 * COUT))
+    step(0, 2)
+    for copy in round_three:
+        copy.wait()
+    packed = jnp.concatenate([stat_all[slot, 0:8] for slot in range(OCT)], axis=0) + between
+    all_cols = columns_of([stat_all[tap // 2, 9 + tap % 2 : 10 + tap % 2] for tap in range(9)])
+    for a in range(3):
+        for c in range(3):
+            window_col[a, c * CIN : (c + 1) * CIN, :] = jnp.broadcast_to(
+                all_cols[:, a * 3 + c : a * 3 + c + 1], (CIN, COUT)
+            )
+
+    step(2, 2)
+    step(1, 3)
+
+    (t0, b0, s0), (t1, b1, s1) = whiten_terms(
+        packed, colors, total_pix, lambda: step(0, 3)
+    )
+    by_x = jnp.concatenate([diag_pair(t0.T, t1.T), diag_pair(b0, b1)], axis=1)
+    by_up = jnp.concatenate([jnp.zeros((COUT, COUT), F32), diag_pair(t0, t1)], axis=1)
+    x_high, up_high = by_x.astype(BF16), by_up.astype(BF16)
+    rhi[0:COUT] = x_high
+    rhi[COUT : 2 * COUT] = x_high
+    rhi[2 * COUT :] = up_high
+    rlo[0:COUT] = (by_x - x_high.astype(F32)).astype(BF16)
+    rlo[COUT:] = (by_up - up_high.astype(F32)).astype(BF16)
+    shift = base[...] - all_mean[:, :COUT]
+    from_up = exact(all_mean[:, COUT:], by_up)
+    level = exact(shift, by_x) - from_up
+    mix[0:COUT] = by_x[:, COUT:]
+    mix[COUT : 2 * COUT] = by_up[:, COUT:]
+    mix[2 * COUT :] = -exact(all_mean[:, :COUT], by_x[:, COUT:]) - from_up[:, COUT:]
+    consts[:, :COUT] = level[:, :COUT] + offset[...]
+    consts[:, COUT:] = level[:, COUT:]
+
+    def spread(block):
+        return jnp.concatenate(
+            [from_right(block).astype(BF16), block.astype(BF16), from_left(block).astype(BF16)],
+            axis=1,
+        )
+
+    def finish(lhs):
+        out = fast(lhs, rhi[...]) + fast(lhs[:, COUT:], rlo[...]) + consts[0:1, :]
+        return out[:, :COUT].astype(BF16), spread(out[:, COUT:])
+
+    def pg_up(b):
+        return remote(
+            pg3.at[b, 1, :, pl.ds(COUT, COUT)],
+            pg_halo.at[1, b],
+            pg_send.at[0, b],
+            pg_recv.at[0, b],
+            up_device,
+        )
+
+    def pg_down(b):
+        return remote(
+            pg3.at[b, BAND, :, pl.ds(COUT, COUT)],
+            pg_halo.at[0, b],
+            pg_send.at[1, b],
+            pg_recv.at[1, b],
+            down_device,
+        )
+
+    @pl.loop(0, IMGS)
+    def _(b):
+        shown, grads = finish(jnp.concatenate([x3[b, 0], x3[b, BAND - 1]], axis=0))
+        colored[b, 0] = shown[:WID]
+        colored[b, BAND - 1] = shown[WID:]
+        pg3[b, 1] = grads[:WID]
+        pg3[b, BAND] = grads[WID:]
+
+        @pl.when(has_up)
+        def _():
+            pg_up(b).start()
+
+        @pl.when(has_down)
+        def _():
+            pg_down(b).start()
+
+    step(1, 4)
+    step(2, 3)
+
+    @pl.loop(0, IMGS)
+    def _(b):
+        shown, grads = finish(x3[b, pl.ds(1, inner)].reshape(inner * WID, 3 * COUT))
+        colored[b, pl.ds(1, inner)] = shown.reshape(inner, WID, COUT)
+        pg3[b, pl.ds(2, inner)] = grads.reshape(inner, WID, ONE_ROW)
+
+    color_grad[0] = s0 * (1.0 / math.sqrt(total_pix))
+    color_grad[1] = s1 * (1.0 / math.sqrt(total_pix))
 
     def image_grad(b):
         lhs = jnp.concatenate(
@@ -625,9 +723,9 @@
         )
         grad_images[b] = fast(lhs, wb[...]).astype(BF16).reshape(BAND, WID, CIN)
 
-    gk[1] = rows_product(0, 1, BAND)
-    step(1, 0)
-    gk[0] = rows_product(0, 2, BAND - 1)
+    step(0, 4)
+    step(1, 5)
+    step(2, 4)
 
     @pl.loop(0, IMGS)
     def _(b):
@@ -636,40 +734,25 @@
             pg_up(b).wait_recv()
             pg3[b, BAND + 1] = spread(pg_halo[1, b].astype(F32))
 
-    gk[0] = gk[0] + rows_product(BAND - 1, BAND + 1, 1)
-    step(0, 0)
-    step(1, 1)
-    gk[2] = rows_product(1, 1, BAND - 1)
-
-    @pl.loop(0, IMGS)
-    def _(b):
         @pl.when(has_up)
         def _():
             pg_down(b).wait_recv()
             pg3[b, 0] = spread(pg_halo[0, b].astype(F32))
 
-    gk[2] = gk[2] + rows_product(0, 0, 1)
-    step(2, 0)
-    step(0, 1)
     image_grad(0)
-    step(2, 1)
     image_grad(1)
-    step(1, 2)
+    step(0, 5)
     image_grad(2)
+    step(1, 6)
     image_grad(3)
-    step(0, 2)
+    step(2, 5)
+    step(1, 7)
     image_grad(4)
-    step(1, 3)
+    step(0, 6)
     image_grad(5)
-    step(2, 2)
-    step(0, 3)
-    step(2, 3)
-    step(1, 4)
-    step(0, 4)
-    step(1, 5)
-    step(2, 4)
-    step(0, 5)
-    step(2, 5)
+    step(0, 7)
+    step(2, 6)
+    step(2, 7)
 
     @pl.loop(0, IMGS)
     def _(b):
@@ -719,7 +802,9 @@
             pltpu.VMEM((3 * ONE_ROW, CIN), BF16),
             pltpu.VMEM((2, GS, GS), F32),
             pltpu.VMEM((1, COUT), F32),
-            pltpu.VMEM((CIN, PIX), BF16),
+            pltpu.VMEM((IMGS, BAND + 2, 3 * CIN, WID), BF16),
+            pltpu.VMEM((BAND + 2, 3, 8, CIN), F32),
+            pltpu.VMEM((3, 3 * CIN, COUT), F32),
             pltpu.VMEM((IMGS, BAND + 2, WID, ONE_ROW), BF16),
             pltpu.VMEM((2, IMGS, WID, COUT), BF16),
             pltpu.VMEM((8, COUT), F32),
@@ -727,16 +812,20 @@
             pltpu.VMEM((COUT, 2 * COUT), F32),
             pltpu.VMEM((3 * COUT, 2 * COUT), BF16),
             pltpu.VMEM((2 * COUT, 2 * COUT), BF16),
+            pltpu.VMEM((2 * COUT + 8, COUT), F32),
             pltpu.VMEM((8, 2 * COUT), F32),
             pltpu.VMEM((OCT, 16, 2 * COUT), F32),
             pltpu.VMEM((OCT, 16, 2 * COUT), F32),
             pltpu.VMEM((PLANE, 16, 2 * COUT), F32),
+            pltpu.VMEM((OCT, 16, 2 * COUT), F32),
             pltpu.VMEM((OCT, 8, 2 * COUT), F32),
-            pltpu.VMEM((3, CIN, ONE_ROW), F32),
-            pltpu.VMEM((3, CIN // 2, ONE_ROW), F32),
-            pltpu.VMEM((3, PLANE - 1, CIN // 32, ONE_ROW), F32),
-            pltpu.VMEM((3, RING, CIN // 32, ONE_ROW), F32),
-            pltpu.VMEM((3, CIN, ONE_ROW), F32),
+            pltpu.VMEM((3, 3 * CIN, 2 * COUT), F32),
+            pltpu.VMEM((3, 3 * CIN // 2, 2 * COUT), F32),
+            pltpu.VMEM((3, RING - 1, 3 * CIN // 8, 2 * COUT), F32),
+            pltpu.VMEM((3, 3 * CIN // 8, 2 * COUT), F32),
+            pltpu.VMEM((3, RING - 1, 3 * CIN // 32, 2 * COUT), F32),
+            pltpu.VMEM((3, RING, 3 * CIN // 32, 2 * COUT), F32),
+            pltpu.VMEM((3, 3 * CIN, COUT), F32),
             dma((IMGS + 1,)),
             dma((11,)),
             dma((2, IMGS)),
@@ -751,13 +840,11 @@
             dma((2, IMGS)),
             dma((3, 2)),
             dma((3, 2)),
-            dma((3, RING - 1)),
-            dma((3, RING - 1)),
-            dma((3, 2, PLANE - 1)),
-            dma((3, 2, PLANE - 1)),
+            dma((3, 5, RING - 1)),
+            dma((3, 5, RING - 1)),
         ],
         compiler_params=pltpu.CompilerParams(
-            collective_id=0, has_side_effects=True, vmem_limit_bytes=40 * 1024 * 1024
+            collective_id=0, has_side_effects=True, vmem_limit_bytes=44 * 1024 * 1024
         ),
     )(
         *[

time: 75.4 us -> 75.3 us (level)
  no operation moved by 1% of the time
where the time goes in v3:
time: 75.3 us; the launch traced here: 75.2 us
  Pallas kernels  74.4 us (99%)
  between operations  0.8 us (1%)
    pallas_call x1, Pallas kernels, body(): pl.pallas_call(functools.partial(block_kernel, total_pix), out_shape=shap...  71.8 us
    pallas_call x1, Pallas kernels, body(): pl.pallas_call(place_kernel, out_shape=shapes, in_specs=[anywhere] * 4, o...  2.61 us

profile of v3, /device:TPU:1, one launch (start us, length us, event | category | flops | bytes accessed | tf_op | source)
XLA Modules:
  0.0 75.2 jit_solution(4345812815675947992)
XLA Ops:
  0.6 71.8 %shard_map.84 = (bf16[6,8,128,128]{3,2,1,0:T(8,128)(2,1)S(1)}, bf16[6,8,128,256]{3,2,1,0:T(8,128)(2,1)S(1)}, f32[3,3,256,128]{3,2,1,0:T(8,128)S(1)}, f32[2,64,64]{2,1,0:T(8,128)S(1)}) custom-call(bf16[6,8,128,256]{3,2,1,0:T(8,128)(2,1)} %images.1, bf16[3,3,256,128]{3,2,1,0:T(8,128)(2,1)} %kernel.1, f32[2,64,64]{2,1,0:T(8,128)} %colors_in.1, ...), custom_call_target="tpu_custom_call" | custom-call | tf_op jit(solution)/shard_map/pallas_call | solution.py:793
  72.4 2.6 %shard_map.85 = (bf16[6,8,128,128]{3,2,1,0:T(8,128)(2,1)}, bf16[6,8,128,256]{3,2,1,0:T(8,128)(2,1)}, f32[3,3,256,128]{3,2,1,0:T(8,128)}, f32[2,64,64]{2,1,0:T(8,128)}) custom-call(bf16[6,8,128,128]{3,2,1,0:T(8,128)(2,1)S(1)} %get-tuple-element.8.refs_0_, bf16[6,8,128,256]{3,2,1,0:T(8,128)(2,1)S(1)} %get-tuple-element.9.refs_1_, ...), custom_call_target="tpu_custom_call" | custom-call | tf_op jit(solution)/shard_map/pallas_call | solution.py:855

commit v4 on v3

--- a/solution.py
+++ b/solution.py
@@ -146,6 +146,7 @@
     rx_second,
     rx_third,
     full,
+    shared,
     load_sem,
     weight_sem,
     halo_send,
@@ -326,12 +327,22 @@
         values = img[b, row].astype(F32)
         for c, moved in enumerate((from_left(values), values, from_right(values))):
             imgt[b, row, c * CIN : (c + 1) * CIN, :] = moved.astype(BF16).T
-            window[row, c] = window[row, c] + moved.reshape(-1, 8, CIN).sum(axis=0)
+
+    lane_row = lax.broadcasted_iota(jnp.int32, (8, CIN), 0)
+
+    def count(b, row):
+        values = img[b, row].astype(F32)
+        total = values.reshape(-1, 8, CIN).sum(axis=0)
+        window[row, 0] = window[row, 0] + (
+            total - jnp.where(lane_row == 7, values[WID - 8 :], 0.0)
+        )
+        window[row, 1] = window[row, 1] + total
+        window[row, 2] = window[row, 2] + (total - jnp.where(lane_row == 0, values[:8], 0.0))
 
     @pl.loop(0, IMGS)
     def _(b):
         for row in range(1, BAND + 1):
-            turn(b, row)
+            count(b, row)
 
     @pl.loop(0, IMGS)
     def _(b):
@@ -358,17 +369,17 @@
         both = absorb(block, ups)
         x3[b, 0, :, : 2 * COUT] = both[:WID]
         x3[b, BAND - 1, :, : 2 * COUT] = both[WID:]
-        turn(b, 0)
-        turn(b, BAND + 1)
-
-    orders = (("x", "y", "z"), ("y", "z", "x"), ("z", "x", "y"))
+        count(b, 0)
+        count(b, BAND + 1)
+
+    orders = (("z", "x", "y"), ("x", "y", "z"), ("y", "z", "x"))
     where = {"x": x, "y": y, "z": z}
     half = 3 * CIN // 2
     quarter = half // RING
     piece = quarter // RING
 
     def rows_at(start, size):
-        return pl.ds(pl.multiple_of(start, 8), size)
+        return pl.ds(pl.multiple_of(start, 32 if size % 32 == 0 else 8), size)
 
     def axis_device(axis, index):
         if axis == "x":
@@ -478,13 +489,14 @@
                 ),
             )
         elif stage == 5:
+            shared[part, my_quarter] = full[part, my_quarter].astype(BF16)
             start(
                 part,
                 line_copies(
                     part,
                     4,
-                    lambda index: full.at[part, my_quarter],
-                    lambda k: full.at[part, my_quarter],
+                    lambda index: shared.at[part, my_quarter],
+                    lambda k: shared.at[part, my_quarter],
                 ),
             )
         elif stage == 6:
@@ -492,8 +504,8 @@
                 part,
                 [
                     remote(
-                        full.at[part, mine],
-                        full.at[part, mine],
+                        shared.at[part, mine],
+                        shared.at[part, mine],
                         gk_core_send.at[part, 1],
                         gk_core_recv.at[part, 1],
                         other_core,
@@ -502,7 +514,7 @@
             )
         elif stage == 7:
             for c in range(3):
-                kernel_grad[part, c] = full[part, c * CIN : (c + 1) * CIN] * (
+                kernel_grad[part, c] = shared[part, c * CIN : (c + 1) * CIN].astype(F32) * (
                     1.0 / math.sqrt(total_pix)
                 )
 
@@ -561,10 +573,11 @@
             rows = slice(c * CIN, (c + 1) * CIN)
             gk[a, rows, :COUT] = gk[a, rows, :COUT] + column * base[0:1, :]
 
-    weight_part(1)
-    step(1, 0)
-    weight_part(0)
-    step(0, 0)
+    @pl.loop(0, IMGS)
+    def _(b):
+        for row in range(BAND + 2):
+            turn(b, row)
+
     for copy in round_one:
         copy.wait()
 
@@ -601,11 +614,13 @@
     ]
     for copy in round_two:
         copy.start()
+    weight_part(1)
+    step(1, 0)
+    weight_part(0)
+    step(0, 0)
     step(1, 1)
     weight_part(2)
     step(2, 0)
-    step(0, 1)
-    step(2, 1)
     for copy in round_two:
         copy.wait()
     rows, tail, means = tails_of(stat_p, PLANE)
@@ -623,10 +638,11 @@
     ]
     for copy in round_three:
         copy.start()
-    step(1, 2)
+    step(0, 1)
+    step(2, 1)
     middle, between = spread_of(means, PIX * OCT)
     all_mean = jnp.broadcast_to(middle, (8, 2 * COUT))
-    step(0, 2)
+    step(1, 2)
     for copy in round_three:
         copy.wait()
     packed = jnp.concatenate([stat_all[slot, 0:8] for slot in range(OCT)], axis=0) + between
@@ -637,11 +653,8 @@
                 all_cols[:, a * 3 + c : a * 3 + c + 1], (CIN, COUT)
             )
 
-    step(2, 2)
-    step(1, 3)
-
     (t0, b0, s0), (t1, b1, s1) = whiten_terms(
-        packed, colors, total_pix, lambda: step(0, 3)
+        packed, colors, total_pix, lambda: (step(0, 2), step(2, 2))
     )
     by_x = jnp.concatenate([diag_pair(t0.T, t1.T), diag_pair(b0, b1)], axis=1)
     by_up = jnp.concatenate([jnp.zeros((COUT, COUT), F32), diag_pair(t0, t1)], axis=1)
@@ -660,6 +673,8 @@
     consts[:, :COUT] = level[:, :COUT] + offset[...]
     consts[:, COUT:] = level[:, COUT:]
 
+    step(1, 3)
+
     def spread(block):
         return jnp.concatenate(
             [from_right(block).astype(BF16), block.astype(BF16), from_left(block).astype(BF16)],
@@ -704,15 +719,15 @@
         def _():
             pg_down(b).start()
 
-    step(1, 4)
-    step(2, 3)
-
-    @pl.loop(0, IMGS)
-    def _(b):
+    def inner_finish(b):
         shown, grads = finish(x3[b, pl.ds(1, inner)].reshape(inner * WID, 3 * COUT))
         colored[b, pl.ds(1, inner)] = shown.reshape(inner, WID, COUT)
         pg3[b, pl.ds(2, inner)] = grads.reshape(inner, WID, ONE_ROW)
 
+    pl.loop(0, IMGS // 2)(inner_finish)
+    step(0, 3)
+    step(2, 3)
+    pl.loop(IMGS // 2, IMGS)(inner_finish)
     color_grad[0] = s0 * (1.0 / math.sqrt(total_pix))
     color_grad[1] = s1 * (1.0 / math.sqrt(total_pix))
 
@@ -723,9 +738,7 @@
         )
         grad_images[b] = fast(lhs, wb[...]).astype(BF16).reshape(BAND, WID, CIN)
 
-    step(0, 4)
-    step(1, 5)
-    step(2, 4)
+    step(1, 4)
 
     @pl.loop(0, IMGS)
     def _(b):
@@ -741,17 +754,20 @@
 
     image_grad(0)
     image_grad(1)
+    step(0, 4)
+    step(2, 4)
+    image_grad(2)
+    step(1, 5)
+    image_grad(3)
+    image_grad(4)
     step(0, 5)
-    image_grad(2)
+    step(2, 5)
+    image_grad(5)
     step(1, 6)
-    image_grad(3)
-    step(2, 5)
     step(1, 7)
-    image_grad(4)
     step(0, 6)
-    image_grad(5)
+    step(2, 6)
     step(0, 7)
-    step(2, 6)
     step(2, 7)
 
     @pl.loop(0, IMGS)
@@ -826,6 +842,7 @@
             pltpu.VMEM((3, RING - 1, 3 * CIN // 32, 2 * COUT), F32),
             pltpu.VMEM((3, RING, 3 * CIN // 32, 2 * COUT), F32),
             pltpu.VMEM((3, 3 * CIN, COUT), F32),
+            pltpu.VMEM((3, 3 * CIN, COUT), BF16),
             dma((IMGS + 1,)),
             dma((11,)),
             dma((2, IMGS)),

time: 75.3 us -> 73 us (0.969)
  Pallas kernels: 74.4 us -> 72.1 us
    pallas_call x1, Pallas kernels: 71.8 us -> 69.5 us  [body(): pl.pallas_call(functools.partial(block_kernel, total_pix), out_shape=shap...]
where the time goes in v4:
time: 73 us; the launch traced here: 72.9 us
  Pallas kernels  72.1 us (99%)
  between operations  0.8 us (1%)
    pallas_call x1, Pallas kernels, body(): pl.pallas_call(functools.partial(block_kernel, total_pix), out_shape=shap...  69.5 us
    pallas_call x1, Pallas kernels, body(): pl.pallas_call(place_kernel, out_shape=shapes, in_specs=[anywhere] * 4, o...  2.61 us

profile of v4, /device:TPU:1, one launch (start us, length us, event | category | flops | bytes accessed | tf_op | source)
XLA Modules:
  0.0 72.9 jit_solution(5490195441388493166)
XLA Ops:
  0.6 69.5 %shard_map.84 = (bf16[6,8,128,128]{3,2,1,0:T(8,128)(2,1)S(1)}, bf16[6,8,128,256]{3,2,1,0:T(8,128)(2,1)S(1)}, f32[3,3,256,128]{3,2,1,0:T(8,128)S(1)}, f32[2,64,64]{2,1,0:T(8,128)S(1)}) custom-call(bf16[6,8,128,256]{3,2,1,0:T(8,128)(2,1)} %images.1, bf16[3,3,256,128]{3,2,1,0:T(8,128)(2,1)} %kernel.1, f32[2,64,64]{2,1,0:T(8,128)} %colors_in.1, ...), custom_call_target="tpu_custom_call" | custom-call | tf_op jit(solution)/shard_map/pallas_call | solution.py:809
  70.1 2.6 %shard_map.85 = (bf16[6,8,128,128]{3,2,1,0:T(8,128)(2,1)}, bf16[6,8,128,256]{3,2,1,0:T(8,128)(2,1)}, f32[3,3,256,128]{3,2,1,0:T(8,128)}, f32[2,64,64]{2,1,0:T(8,128)}) custom-call(bf16[6,8,128,128]{3,2,1,0:T(8,128)(2,1)S(1)} %get-tuple-element.8.refs_0_, bf16[6,8,128,256]{3,2,1,0:T(8,128)(2,1)S(1)} %get-tuple-element.9.refs_1_, ...), custom_call_target="tpu_custom_call" | custom-call | tf_op jit(solution)/shard_map/pallas_call | solution.py:872
